TPU v7x, 256 devices: a whole 4x4x8 slice. The times are simulated.
256 devices in a mesh: wide: 32 (over x, y, core), narrow: 8 (over z).
Axes of the slice: x: 4, y: 4, z: 8, core: 2. Of those that a mesh axis runs over, the one named last changes fastest.
Arguments:
- embeddings: bfloat16 [524288, 1536], P(('wide', 'narrow')), may hold values from -6 to 6
- point_counts: int32 [524288], P(('wide', 'narrow')), may hold values from 1 to 64
- owner_ids: int32 [524288, 1], P(('wide', 'narrow')), may hold values from 0 to 255; in each aligned block of 2048 rows (0 to 2047, 2048 to 4095, ...) at most 16 rows name the same one
- owner_slots: int32 [524288, 1], P(('wide', 'narrow')), may hold values from 0 to 255
- reseed_slots: int32 [256, 2], P(('wide', 'narrow')), may hold values from 0 to 255, as said below
- donor_ids: int32 [256, 2], P(('wide', 'narrow')), may hold values from 0 to 524287
- parents_two: int32 [65536], P(('wide', 'narrow')), may hold values from 0 to 1023
- parents_three: int32 [1024], P('narrow'), may hold values from 0 to 255
Outputs:
- level_two: float32 [65536, 1536], P(('wide', 'narrow'))
- level_three: float32 [1024, 1536], P('narrow')
- level_four: float32 [256, 1536], replicated
Inputs may be any that keep to these rules, and one draw needn't show every extreme that they name: `owner_ids`: among the level-1 centroids of one device at most 16 have their parent on one owner, and some owner has exactly 16. `reseed_slots`: the entries of one device's row are different.
All inputs are finite; a program needn't handle non-finite values.
Results may differ from a plain program's by a relative error of at most 0.0003.
Values may be sent and summed in bfloat16 or wider, within the bound.
A program may use at most 128 MiB of HBM per device.

v0:
```python
import jax
import jax.numpy as jnp
from jax import lax
from jax.sharding import PartitionSpec as P

L4 = 256


def per_device(
    embeddings,
    point_counts,
    owner_ids,
    owner_slots,
    reseed_slots,
    donor_ids,
    parents_two,
    parents_three,
):
    wide_count = lax.axis_size("wide")
    narrow_count = lax.axis_size("narrow")
    device_total = wide_count * narrow_count
    rows_local, feature_width = embeddings.shape
    clusters = parents_two.shape[0]
    capacity = max(2, 2 * rows_local // device_total)
    targets = owner_ids[:, 0]
    marker = (targets[:, None] == jnp.arange(device_total, dtype=jnp.int32)[None, :]).astype(
        jnp.int32
    )
    earlier = jnp.cumsum(marker, axis=0) - marker
    ranking = jnp.sum(earlier * marker, axis=1)
    position = targets * capacity + ranking
    outgoing = (
        jnp.zeros((device_total * capacity, feature_width), jnp.bfloat16)
        .at[position]
        .set(embeddings)
    )
    outgoing = outgoing.reshape(wide_count, narrow_count, capacity, feature_width)
    labels = jnp.stack(
        [owner_slots[:, 0].astype(jnp.float32), point_counts.astype(jnp.float32)], axis=1
    ).astype(jnp.bfloat16)
    out_labels = jnp.zeros((device_total * capacity, 2), jnp.bfloat16).at[position].set(labels)
    out_labels = out_labels.reshape(wide_count, narrow_count, capacity, 2)
    incoming, in_labels = (
        lax.all_to_all(
            lax.all_to_all(outgoing, "wide", split_axis=0, concat_axis=0, tiled=True),
            "narrow",
            split_axis=1,
            concat_axis=1,
            tiled=True,
        ),
        lax.all_to_all(
            lax.all_to_all(out_labels, "wide", split_axis=0, concat_axis=0, tiled=True),
            "narrow",
            split_axis=1,
            concat_axis=1,
            tiled=True,
        ),
    )
    incoming = incoming.reshape(-1, feature_width)
    in_labels = in_labels.reshape(-1, 2)
    member_slot = in_labels[:, 0].astype(jnp.int32)
    member_weight = in_labels[:, 1]
    matches = member_slot[None, :] == jnp.arange(clusters, dtype=jnp.int32)[:, None]
    assign_two = jnp.where(matches, member_weight[None, :], jnp.zeros((), jnp.bfloat16))
    sums_two = jnp.dot(assign_two, incoming, preferred_element_type=jnp.float32)
    weight_two = jnp.sum(assign_two.astype(jnp.float32), axis=1)
    centre_two = sums_two / jnp.maximum(weight_two, 1.0)[:, None]
    requests = lax.all_gather(donor_ids[0], ("wide", "narrow"), axis=0, tiled=True)
    first_row = lax.axis_index(("wide", "narrow")) * rows_local
    local_row = requests - first_row
    inside = (local_row >= 0) & (local_row < rows_local)
    picked = embeddings[jnp.clip(local_row, 0, rows_local - 1)].astype(jnp.float32)
    donor_rows = lax.psum_scatter(
        jnp.where(inside[:, None], picked, 0.0), ("wide", "narrow"), scatter_dimension=0, tiled=True
    )
    centre_two = centre_two.at[reseed_slots[0]].set(donor_rows)
    per_owner = parents_three.shape[0]
    total_three = per_owner * narrow_count
    rows_three = jnp.arange(total_three, dtype=jnp.int32)
    assign_three = jnp.where(parents_two[None, :] == rows_three[:, None], weight_two[None, :], 0.0)
    partial_value = jnp.dot(
        assign_three,
        centre_two,
        precision=lax.Precision.HIGHEST,
        preferred_element_type=jnp.float32,
    )
    masses = jnp.sum(assign_three, axis=1)
    partial_value, masses = (
        lax.psum_scatter(partial_value, "narrow", scatter_dimension=0, tiled=True),
        lax.psum_scatter(masses, "narrow", scatter_dimension=0, tiled=True),
    )
    sums_three, weight_three = lax.psum((partial_value, masses), "wide")
    centre_three = sums_three / jnp.maximum(weight_three, 1.0)[:, None]
    assign_four = jnp.where(
        parents_three[None, :] == jnp.arange(L4, dtype=jnp.int32)[:, None],
        weight_three[None, :],
        0.0,
    )
    sums_four = jnp.dot(
        assign_four,
        centre_three,
        precision=lax.Precision.HIGHEST,
        preferred_element_type=jnp.float32,
    )
    mass_four = jnp.sum(assign_four, axis=1)
    sums_four, mass_four = lax.psum((sums_four, mass_four), "narrow")
    centre_four = sums_four / jnp.maximum(mass_four, 1.0)[:, None]
    return (centre_two, centre_three, centre_four)


def solution(mesh):
    in_specs = (
        P(("wide", "narrow"), None),
        P(("wide", "narrow")),
        P(("wide", "narrow"), None),
        P(("wide", "narrow"), None),
        P(("wide", "narrow"), None),
        P(("wide", "narrow"), None),
        P(("wide", "narrow")),
        P("narrow"),
    )
    out_specs = (P(("wide", "narrow"), None), P("narrow", None), P())
    return jax.shard_map(
        per_device, mesh=mesh, in_specs=in_specs, out_specs=out_specs, check_vma=False
    )
```

profile of v0, /device:TPU:1, one launch (start us, length us, event | category | flops | bytes accessed | tf_op | source)
XLA Modules:
  0.0 1152.4 jit_solution(4462253980848217439)
XLA Ops:
  7.2 0.8 copy.43
  8.0 0.3 fusion.11
  8.4 0.2 broadcast_add_fusion
  8.6 0.0 copy-start.2
  8.6 1.2 copy.44
  9.8 0.0 copy-start.4
  9.8 0.0 copy-start.5
  9.9 0.9 fusion.9
  10.9 0.3 copy.45
  11.3 6.1 scatter_custom_fusion
  17.3 1.6 copy.46
  18.9 0.8 reshape.153
  19.7 8.6 all-to-all-start
  28.3 18.0 %scatter_custom_fusion.1 = bf16[4096,1536]{1,0:T(8,128)(2,1)} fusion(s32[2048]{0:T(1024)S(1)} %bitcast.49, bf16[2048,1536]{1,0:T(8,128)(2,1)} %param.8, bf16[]{:T(256)} %constant.13.clone.1), kind=kCustom, calls=%fused_computation.4 | custom fusion | bytes 12583424 | tf_op jit(solution)/shard_map/scatter | solution.py:35
  46.3 0.0 all-to-all-done
  46.3 7.4 all-to-all-start.2
  53.7 0.1 reshape.154
  53.9 0.2 copy.47
  54.1 0.7 reshape.155
  54.8 173.6 %all-to-all-done.2 = bf16[32,8,16,1536]{3,2,1,0:T(8,128)(2,1)} async-done(((bf16[32,8,16,1536]{3,2,1,0:T(8,128)(2,1)}), bf16[32,8,16,1536]{3,2,1,0:T(8,128)(2,1)}, u32[]{:S(2)}, u32[]{:S(2)}) %all-to-all-start.2) | async-done | bytes 12582944 | tf_op jit(solution)/shard_map/all_to_all | solution.py:45
  228.4 8.2 all-to-all-start.1
  236.6 10.9 copy.49
  247.5 0.0 all-to-all-done.1
  247.5 6.8 all-to-all-start.3
  254.3 0.0 all-reduce.11.cloned.1.call-start
  254.3 0.1 bitcast_dynamic-update-slice_fusion
  254.4 339.9 %all-reduce = s32[512]{0:T(512)S(1)} all-reduce(s32[512]{0:T(512)S(1)} %bitcast_dynamic-update-slice_fusion), channel_id=2, replica_groups=mesh['wide'=32,'narrow'=8] {'wide','narrow'}, use_global_device_ids=true, to_apply=%add | all-reduce | flops 512 | bytes 4096
  594.3 7.2 gather_fusion
  601.5 2.0 convert_select_fusion
  603.6 0.0 all-reduce.11.cloned.1.call-update
  603.6 0.3 reduce-scatter.2.cloned.1.call-start
  603.9 0.4 copy-done.8
  604.2 0.1 reshape.156
  604.3 0.1 copy.48
  604.5 0.2 reshape.83
  604.6 0.1 slice_reduce_fusion
  604.7 0.6 convert_reduce_fusion
  605.4 6.4 copy.50
  611.8 0.0 copy-start.3
  611.8 3.5 fusion.5
  615.3 248.8 %all-reduce.11.cloned.1.call-done = f32[512,1536]{1,0:T(8,128)} async-done(((f32[512,1536]{1,0:T(8,128)}), f32[512,1536]{1,0:T(8,128)}) %all-reduce.11.cloned.1.call-update) | async-done | bytes 3145744
  864.1 1.5 scatter_custom_fusion.2
  865.5 0.0 copy-start.1
  865.6 7.2 fusion.13
  872.7 0.0 reduce-scatter.2.cloned.1.call-update
  872.7 0.0 copy-start.6
  872.7 0.0 all-reduce.7.cloned.1.call-start
  872.8 75.5 %reduce-scatter.2.cloned.1.call-done = f32[128,1536]{1,0:T(8,128)} async-done(((f32[1024,1536]{1,0:T(8,128)}), f32[128,1536]{1,0:T(8,128)}) %reduce-scatter.2.cloned.1.call-update) | async-done | bytes 786448 | tf_op jit(solution)/shard_map/reduce_scatter | solution.py:89
  948.3 0.0 all-reduce.7.cloned.1.call-update
  948.3 0.0 all-reduce.9.cloned.1.call-start
  948.4 0.6 dynamic-slice.1
  949.6 0.2 select_reduce_fusion
  949.9 11.9 %all-reduce.2 = f32[1024]{0:T(1024)S(1)} all-reduce(f32[1024]{0:T(1024)S(1)} %select_reduce_fusion), channel_id=5, replica_groups=mesh['wide'=32,'narrow'=8] {'narrow'}, use_global_device_ids=true, to_apply=%region_11.12.clone | all-reduce | flops 1024 | bytes 8192
  961.8 0.1 dynamic-slice.2
  961.8 66.3 %psum.29 = f32[128]{0:T(128)S(1)} all-reduce(f32[128]{0:T(128)S(1)} %dynamic-slice.2), channel_id=1, replica_groups=mesh['wide'=32,'narrow'=8] {'wide'}, use_global_device_ids=true, to_apply=%region_12.13 | all-reduce | flops 128 | bytes 1024 | tf_op jit(solution)/shard_map/psum | solution.py:92
  1028.1 36.2 %all-reduce.7.cloned.1.call-done = f32[128,1536]{1,0:T(8,128)} async-done(((f32[128,1536]{1,0:T(8,128)}), f32[128,1536]{1,0:T(8,128)}) %all-reduce.7.cloned.1.call-update) | async-done | bytes 786448 | tf_op jit(solution)/shard_map/psum | solution.py:92
  1064.4 1.3 broadcast_divide_fusion.1
  1065.6 0.0 copy-start
  1065.7 2.6 fusion.23
  1068.2 0.0 all-reduce.9.cloned.1.call-update
  1068.2 0.1 select_reduce_fusion.1
  1068.3 13.7 %psum.31 = f32[256]{0:T(256)S(1)} all-reduce(f32[256]{0:T(256)S(1)} %select_reduce_fusion.1), channel_id=1, replica_groups=mesh['wide'=32,'narrow'=8] {'narrow'}, use_global_device_ids=true, to_apply=%region_15.16 | all-reduce | flops 256 | bytes 2048 | tf_op jit(solution)/shard_map/psum | solution.py:106
  1082.1 61.0 %all-reduce.9.cloned.1.call-done = f32[256,1536]{1,0:T(8,128)} async-done(((f32[256,1536]{1,0:T(8,128)}), f32[256,1536]{1,0:T(8,128)}) %all-reduce.9.cloned.1.call-update) | async-done | bytes 1572880 | tf_op jit(solution)/shard_map/psum | solution.py:106
  1143.1 2.8 broadcast_divide_fusion
  (29 shorter events, 0.2 us)
Async XLA Ops:
  8.6 1.3 copy-start.2
  9.8 1.0 copy-start.4
  9.8 1.0 copy-start.5
  19.7 26.6 %all-to-all-start = ((bf16[32,2,128]{2,1,0:T(2,128)(2,1)}), bf16[32,2,128]{2,1,0:T(2,128)(2,1)S(1)}, u32[]{:S(2)}, u32[]{:S(2)}) async-start(bf16[32,2,128]{2,1,0:T(2,128)(2,1)} %reshape.153), calls=%async_computation | async-start | bytes 32768 | tf_op jit(solution)/shard_map/all_to_all | solution.py:52
  46.3 182.1 %all-to-all-start.2 = ((bf16[32,8,16,1536]{3,2,1,0:T(8,128)(2,1)}), bf16[32,8,16,1536]{3,2,1,0:T(8,128)(2,1)}, u32[]{:S(2)}, u32[]{:S(2)}) async-start(bf16[32,8,16,1536]{3,2,1,0:T(8,128)(2,1)} %bitcast.36), calls=%async_computation.2 | async-start | bytes 25165824 | tf_op jit(solution)/shard_map/all_to_all | solution.py:45
  228.4 19.1 %all-to-all-start.1 = ((bf16[8,2,512]{2,1,0:T(2,128)(2,1)}), bf16[8,2,512]{2,1,0:T(2,128)(2,1)S(1)}, u32[]{:S(2)}, u32[]{:S(2)}) async-start(bf16[8,2,512]{2,1,0:T(2,128)(2,1)} %reshape.155), calls=%async_computation.1 | async-start | bytes 32768 | tf_op jit(solution)/shard_map/all_to_all | solution.py:51
  247.5 6.8 copy-start.7
  247.5 357.9 %all-to-all-start.3 = ((bf16[32,8,16,1536]{3,2,0,1:T(8,128)(2,1)}), bf16[32,8,16,1536]{3,2,0,1:T(8,128)(2,1)}, u32[]{:S(2)}, u32[]{:S(2)}) async-start(bf16[32,8,16,1536]{3,2,0,1:T(8,128)(2,1)} %copy.49), calls=%async_computation.3 | async-start | bytes 25165824 | tf_op jit(solution)/shard_map/all_to_all | solution.py:44
  254.3 609.8 %all-reduce.11.cloned.1.call-start = ((), (), s32[]{:S(2)}) async-start(), calls=%async_computation.8 | async-start | bytes 6291456
  603.6 0.7 copy-start.8
  603.6 344.7 %reduce-scatter.2.cloned.1.call-start = ((), (), s32[]{:S(2)}) async-start(), calls=%async_computation.5 | async-start | bytes 7077888 | tf_op jit(solution)/shard_map/reduce_scatter | solution.py:89
  611.8 253.7 %copy-start.3 = (s32[256]{0:T(256)S(1)}, s32[256]{0:T(256)}, u32[]{:S(2)}) copy-start(s32[256]{0:T(256)} %param.14) | copy-start | bytes 3076
  865.5 7.2 copy-start.1
  872.7 75.7 %copy-start.9 = (u32[256]{0:T(256)S(1)}, u32[256]{0:T(256)}, u32[]{:S(2)}) copy-start(u32[256]{0:T(256)} %constant.51) | copy-start | bytes 3076
  872.7 192.9 %copy-start.6 = (s32[128]{0:T(128)S(1)}, s32[128]{0:T(128)}, u32[]{:S(2)}) copy-start(s32[128]{0:T(128)} %param.15) | copy-start | bytes 1540
  872.7 191.6 %all-reduce.7.cloned.1.call-start = ((), (), s32[]{:S(2)}) async-start(), calls=%async_computation.6 | async-start | bytes 1572864 | tf_op jit(solution)/shard_map/psum | solution.py:92
  948.3 194.7 %all-reduce.9.cloned.1.call-start = ((), (), s32[]{:S(2)}) async-start(), calls=%async_computation.7 | async-start | bytes 3145728 | tf_op jit(solution)/shard_map/psum | solution.py:106
  1065.6 80.2 %copy-start = (f32[128,1536]{1,0:T(8,128)}, f32[128,1536]{1,0:T(8,128)S(1)}, u32[]{:S(2)}) copy-start(f32[128,1536]{1,0:T(8,128)S(1)} %broadcast_divide_fusion.1) | copy-start | bytes 2359300
Sparse Core Ops, SparseCore 0:
  603.7 260.2 all-reduce.10
  872.9 75.4 reduce-scatter.1
  951.9 112.4 all-reduce.6
  1068.4 74.6 all-reduce.8
where the time goes:
time: 1160 us; the launch traced here: 1150 us
  waiting for transfers between devices  595 us (51%)
  blocking collectives  432 us (37%)
  local copies, waits for them, and re-layouts  57.4 us (5%)
  starting transfers between devices  31.4 us (3%)
  between operations  14.7 us (1%)
  matrix products  13.2 us (1%)
    unnamed x2, blocking collectives  352 us
    unnamed x5, waiting for transfers between devices  249 us
    all_to_all x1, waiting for transfers between devices, per_device(): lax.all_to_all(outgoing, 'wide', split_axis=0, concat_axis=0, tiled=True)  174 us
    reduce_scatter x1, waiting for transfers between devices, per_device(): lax.psum_scatter(partial_value, 'narrow', scatter_dimension=0, tiled=True)  75.5 us
    psum x1, blocking collectives, per_device(): sums_three, weight_three = lax.psum((partial_value, masses), 'wide')  66.3 us
    psum x1, waiting for transfers between devices, per_device(): sums_four, mass_four = lax.psum((sums_four, mass_four), 'narrow')  61 us
    psum x1, waiting for transfers between devices, per_device(): sums_three, weight_three = lax.psum((partial_value, masses), 'wide')  36.2 us
  transfers between devices with their start and end apart: 8, of which 5 were waited for; matrix products, arithmetic and copies ran while one was open for 4% of the time, Pallas kernels for 0%

commit v1 on v0

v1 whole, which is shorter than its diff:
```python
import functools

import jax
import jax.numpy as jnp
from jax import lax
from jax.experimental import pallas as pl
from jax.experimental.pallas import tpu as pltpu
from jax.sharding import PartitionSpec as P

L4 = 256
CAP = 16
NX, NY, NC, NZ = 4, 4, 2, 8
NW = NX * NY * NC
MESH = pl.DeviceIdType.MESH
SEND_BUFFERS = 3

XY_ORDER = [
    (1, 0), (0, 1), (3, 0), (0, 3), (2, 2), (1, 1), (3, 3), (1, 3),
    (3, 1), (2, 0), (0, 2), (2, 1), (1, 2), (2, 3), (3, 2),
]
WIDE_ORDER = [(dx, dy, dc) for dc in range(NC) for dx, dy in XY_ORDER] + [(0, 0, 1)]


def nt_dot(a, b):
    return lax.dot_general(
        a, b, (((1,), (1,)), ((), ())), preferred_element_type=jnp.float32
    )


def iota(shape, axis):
    return lax.broadcasted_iota(jnp.int32, shape, axis)


def exchange_kernel(
    emb, own, slot, cnt,
    out, weight_out,
    sbuf, rbuf, onehot, pos, lab_send, lab_recv, lab_t, ring_f, ring_b, w_send, w_recv,
    s_sem, r_sem, lab_sems, f_send, f_recv, b_send, b_recv, w_sems,
):
    rows, width = emb.shape
    half = width // 2
    w = lax.axis_index("wide")
    z = lax.axis_index("narrow")
    x, y, c = w // 8, (w // 2) % 4, w % 2

    def wide_peer(d):
        return (((x + d[0]) % NX) * 8 + ((y + d[1]) % NY) * 2 + (c + d[2]) % NC, z)

    def z_peer(k):
        return (w, (z + k) % NZ)

    barrier = pltpu.get_barrier_semaphore()
    for d in WIDE_ORDER:
        pl.semaphore_signal(barrier, inc=1, device_id=wide_peer(d), device_id_type=MESH)
    for k in range(1, NZ):
        pl.semaphore_signal(barrier, inc=1, device_id=z_peer(k), device_id_type=MESH)

    owner = own[...]
    target = owner // NZ
    rel = (
        ((target // 8 - x) & 3) * 8 + (((target // 2) - y) & 3) * 2 + ((target - c) & 1)
    )
    step = 256
    upper = (iota((step, step), 0) < iota((step, step), 1)).astype(jnp.bfloat16)
    carry = jnp.zeros((step, 1), jnp.float32)
    for b in range(rows // step):
        cols = slice(b * step, (b + 1) * step)
        hit = iota((step, step), 0) == owner[:, cols]
        mark = hit.astype(jnp.bfloat16)
        earlier = jnp.dot(mark, upper, preferred_element_type=jnp.float32) + carry
        mark32 = hit.astype(jnp.float32)
        rank = jnp.sum(earlier * mark32, axis=0, keepdims=True)
        carry = carry + jnp.sum(mark32, axis=1, keepdims=True)
        pos[0:1, cols] = rel[:, cols] * CAP + rank.astype(jnp.int32)
    pos[1:2, :] = owner % NZ

    places = NW * CAP
    tile = 256

    def fill_onehot(where_row):
        for i in range(places // tile):
            ids = iota((tile, rows), 0) + i * tile
            onehot[i * tile : (i + 1) * tile, :] = (ids == where_row).astype(jnp.bfloat16)

    fill_onehot(pos[0:1, :])
    lane = iota((128, rows), 0)
    z_of = pos[1:2, :]
    labels = jnp.where(
        lane == 2 * z_of, slot[...], jnp.where(lane == 2 * z_of + 1, cnt[...], 0)
    ).astype(jnp.float32).astype(jnp.bfloat16)
    lab_send[...] = nt_dot(onehot[...], labels).astype(jnp.bfloat16)
    lab_recv[0:CAP, :] = lab_send[0:CAP, :]

    pl.semaphore_wait(barrier, NW - 1 + NZ - 1)

    def send_wide(src, dst, sem_s, sem_r):
        for d in WIDE_ORDER:
            k = d[0] * 8 + d[1] * 2 + d[2]
            at = pl.ds(k * CAP, CAP)
            pltpu.make_async_remote_copy(
                src_ref=src.at[at], dst_ref=dst.at[at], send_sem=sem_s, recv_sem=sem_r,
                device_id=wide_peer(d), device_id_type=MESH,
            ).start()

    def all_wide(src, dst, sem_s, sem_r):
        at = pl.ds(CAP, places - CAP)
        return pltpu.make_async_remote_copy(
            src_ref=src.at[at], dst_ref=dst.at[at], send_sem=sem_s, recv_sem=sem_r,
            device_id=wide_peer((0, 0, 1)), device_id_type=MESH,
        )

    send_wide(lab_send, lab_recv, lab_sems.at[0], lab_sems.at[1])

    def block_f(t):
        return (z + 2 * NZ - 1 - t) % NZ

    def block_b(t):
        return (z + 1 + t) % NZ

    def pack_and_send(t):
        b = lax.rem(t, SEND_BUFFERS)

        @pl.when(t >= SEND_BUFFERS)
        def _():
            all_wide(sbuf.at[b], rbuf.at[t], s_sem.at[b], r_sem.at[t]).wait_send()

        for h, blk in enumerate((block_f(t), block_b(t))):
            fill_onehot(jnp.where(pos[1:2, :] == blk, pos[0:1, :], -1))

            def column(n, _, h=h):
                at = pl.ds(pl.multiple_of(h * half + n * tile, tile), tile)
                sbuf[b, :, at] = jnp.dot(
                    onehot[...], emb[:, at], preferred_element_type=jnp.float32
                ).astype(jnp.bfloat16)
                return 0

            lax.fori_loop(0, half // tile, column, 0)
        rbuf[t, 0:CAP, :] = sbuf[b, 0:CAP, :]
        send_wide(sbuf.at[b], rbuf.at[t], s_sem.at[b], r_sem.at[t])

    pack_and_send(0)

    all_wide(lab_send, lab_recv, lab_sems.at[0], lab_sems.at[1]).wait()
    eye = (iota((16, 128), 0) == iota((16, 128), 1)).astype(jnp.bfloat16)
    lab_t[...] = nt_dot(eye, lab_recv[...])
    clusters = out.shape[0]

    def matched(blk):
        ids = iota((clusters, places), 0).astype(jnp.float32)
        return ids == lab_t[pl.ds(2 * blk, 1), :], lab_t[pl.ds(2 * blk + 1, 1), :]

    def weigh(k, _):
        hit, counts = matched((z + k) % NZ)
        counts = jnp.broadcast_to(counts, (8, places)).astype(jnp.bfloat16)
        w_send[k] = nt_dot(counts, hit.astype(jnp.float32).astype(jnp.bfloat16))
        return 0

    lax.fori_loop(0, NZ, weigh, 0)

    def weight_copy(src, dst, k):
        return pltpu.make_async_remote_copy(
            src_ref=src, dst_ref=dst, send_sem=w_sems.at[0], recv_sem=w_sems.at[1],
            device_id=z_peer(k), device_id_type=MESH,
        )

    for k in range(1, NZ):
        weight_copy(w_send.at[k], w_recv.at[k], k).start()

    def ring_copy(ring, t, sems, k):
        return pltpu.make_async_remote_copy(
            src_ref=ring.at[t], dst_ref=ring.at[t + 1],
            send_sem=sems[0].at[t], recv_sem=sems[1].at[t + 1],
            device_id=z_peer(k), device_id_type=MESH,
        )

    rings = (
        (ring_f, (f_send, f_recv), 1, block_f),
        (ring_b, (b_send, b_recv), NZ - 1, block_b),
    )

    def reduce_stage(t):
        all_wide(sbuf.at[0], rbuf.at[t], s_sem.at[0], r_sem.at[t]).wait_recv()
        for h, (ring, sems, k, block) in enumerate(rings):
            hit, counts = matched(block(t))
            assign = jnp.where(hit, counts, 0.0).astype(jnp.bfloat16)

            @pl.when(t > 0)
            def _(ring=ring, sems=sems, k=k):
                ring_copy(ring, t - 1, sems, k).wait_recv()

            for n in range(half // tile):
                at = slice(n * tile, (n + 1) * tile)
                part = jnp.dot(
                    assign,
                    rbuf[t, :, h * half + n * tile : h * half + (n + 1) * tile],
                    preferred_element_type=jnp.float32,
                )

                @pl.when(t == 0)
                def _(ring=ring, at=at, part=part):
                    ring[t, :, at] = part

                @pl.when(t > 0)
                def _(ring=ring, at=at, part=part):
                    ring[t, :, at] += part

            @pl.when(t < NZ - 1)
            def _(ring=ring, sems=sems, k=k):
                ring_copy(ring, t, sems, k).start()

    def stage(t, _):
        @pl.when(t < NZ - 1)
        def _():
            pack_and_send(t + 1)

        reduce_stage(t)
        return 0

    lax.fori_loop(0, NZ, stage, 0)

    others = pl.ds(1, NZ - 1)
    weight_copy(w_send.at[others], w_recv.at[others], 1).wait()
    total = w_send[0]
    for k in range(1, NZ):
        total = total + w_recv[k]
    weight_out[...] = total
    diagonal = iota((clusters, clusters), 0) == iota((clusters, clusters), 1)
    column_w = jnp.sum(jnp.where(diagonal, total[0:1, :], 0.0), axis=1, keepdims=True)
    column_w = jnp.maximum(column_w, 1.0)
    for h, (ring, sems, k, block) in enumerate(rings):
        for n in range(half // tile):
            at = slice(n * tile, (n + 1) * tile)
            out[:, h * half + n * tile : h * half + (n + 1) * tile] = (
                ring[NZ - 1, :, at] / column_w
            )

    for b in range(SEND_BUFFERS):
        all_wide(sbuf.at[b], rbuf.at[0], s_sem.at[b], r_sem.at[0]).wait_send()
    for ring, sems, k, block in rings:
        def drain(t, _, ring=ring, sems=sems, k=k):
            ring_copy(ring, t, sems, k).wait_send()
            return 0

        lax.fori_loop(0, NZ - 1, drain, 0)


def exchange(embeddings, owner_ids, owner_slots, point_counts, clusters):
    rows, width = embeddings.shape
    places = NW * CAP
    vmem = pl.BlockSpec(memory_space=pltpu.VMEM)
    dma = pltpu.SemaphoreType.DMA
    return pl.pallas_call(
        exchange_kernel,
        out_shape=(
            jax.ShapeDtypeStruct((clusters, width), jnp.float32),
            jax.ShapeDtypeStruct((8, clusters), jnp.float32),
        ),
        in_specs=[vmem] * 4,
        out_specs=(vmem, vmem),
        scratch_shapes=[
            pltpu.VMEM((SEND_BUFFERS, places, width), jnp.bfloat16),
            pltpu.VMEM((NZ, places, width), jnp.bfloat16),
            pltpu.VMEM((places, rows), jnp.bfloat16),
            pltpu.VMEM((8, rows), jnp.int32),
            pltpu.VMEM((places, 128), jnp.bfloat16),
            pltpu.VMEM((places, 128), jnp.bfloat16),
            pltpu.VMEM((16, places), jnp.float32),
            pltpu.VMEM((NZ, clusters, width // 2), jnp.float32),
            pltpu.VMEM((NZ, clusters, width // 2), jnp.float32),
            pltpu.VMEM((NZ, 8, clusters), jnp.float32),
            pltpu.VMEM((NZ, 8, clusters), jnp.float32),
            dma((SEND_BUFFERS,)),
            dma((NZ,)),
            dma((2,)),
            dma((NZ,)),
            dma((NZ,)),
            dma((NZ,)),
            dma((NZ,)),
            dma((2,)),
        ],
        compiler_params=pltpu.CompilerParams(
            collective_id=0, has_side_effects=True, vmem_limit_bytes=60 * 2**20
        ),
    )(
        embeddings,
        owner_ids.reshape(1, rows),
        owner_slots.reshape(1, rows),
        point_counts.reshape(1, rows),
    )


def per_device(
    embeddings,
    point_counts,
    owner_ids,
    owner_slots,
    reseed_slots,
    donor_ids,
    parents_two,
    parents_three,
):
    narrow_count = lax.axis_size("narrow")
    rows_local, feature_width = embeddings.shape
    clusters = parents_two.shape[0]
    requests = lax.all_gather(donor_ids[0], ("wide", "narrow"), axis=0, tiled=True)
    first_row = lax.axis_index(("wide", "narrow")) * rows_local
    local_row = requests - first_row
    inside = (local_row >= 0) & (local_row < rows_local)
    picked = embeddings[jnp.clip(local_row, 0, rows_local - 1)].astype(jnp.float32)
    donor_rows = lax.psum_scatter(
        jnp.where(inside[:, None], picked, 0.0), ("wide", "narrow"), scatter_dimension=0, tiled=True
    )
    centre_two, weight_rows = exchange(
        embeddings, owner_ids, owner_slots, point_counts, clusters
    )
    weight_two = weight_rows[0]
    centre_two = centre_two.at[reseed_slots[0]].set(donor_rows)
    per_owner = parents_three.shape[0]
    total_three = per_owner * narrow_count
    rows_three = jnp.arange(total_three, dtype=jnp.int32)
    assign_three = jnp.where(parents_two[None, :] == rows_three[:, None], weight_two[None, :], 0.0)
    partial_value = jnp.dot(
        assign_three,
        centre_two,
        precision=lax.Precision.HIGHEST,
        preferred_element_type=jnp.float32,
    )
    masses = jnp.sum(assign_three, axis=1)
    partial_value, masses = (
        lax.psum_scatter(partial_value, "narrow", scatter_dimension=0, tiled=True),
        lax.psum_scatter(masses, "narrow", scatter_dimension=0, tiled=True),
    )
    sums_three, weight_three = lax.psum((partial_value, masses), "wide")
    centre_three = sums_three / jnp.maximum(weight_three, 1.0)[:, None]
    assign_four = jnp.where(
        parents_three[None, :] == jnp.arange(L4, dtype=jnp.int32)[:, None],
        weight_three[None, :],
        0.0,
    )
    sums_four = jnp.dot(
        assign_four,
        centre_three,
        precision=lax.Precision.HIGHEST,
        preferred_element_type=jnp.float32,
    )
    mass_four = jnp.sum(assign_four, axis=1)
    sums_four, mass_four = lax.psum((sums_four, mass_four), "narrow")
    centre_four = sums_four / jnp.maximum(mass_four, 1.0)[:, None]
    return (centre_two, centre_three, centre_four)


def solution(mesh):
    in_specs = (
        P(("wide", "narrow"), None),
        P(("wide", "narrow")),
        P(("wide", "narrow"), None),
        P(("wide", "narrow"), None),
        P(("wide", "narrow"), None),
        P(("wide", "narrow"), None),
        P(("wide", "narrow")),
        P("narrow"),
    )
    out_specs = (P(("wide", "narrow"), None), P("narrow", None), P())
    return jax.shard_map(
        per_device, mesh=mesh, in_specs=in_specs, out_specs=out_specs, check_vma=False
    )
```

time: 1160 us -> 673 us (0.58)
  waiting for transfers between devices: 595 us -> 277 us
  blocking collectives: 432 us -> 173 us
  Pallas kernels: 0 us -> 174 us
  local copies, waits for them, and re-layouts: 57.4 us -> 13.9 us
  starting transfers between devices: 31.4 us -> 0.16 us
    unnamed x2, blocking collectives: 352 us -> 93.3 us
    pallas_call x0 -> x1, Pallas kernels: none -> 174 us  [exchange(): pl.pallas_call(exchange_kernel, out_shape=(jax.ShapeDtypeStruct((clusters...]
    all_to_all x4 -> x0, waiting for transfers between devices: 174 us -> none  [the longest x1 174 us: per_device(): lax.all_to_all(outgoing, 'wide', split_axis=0, concat_axis=0, tiled=True)]
    unnamed x5, waiting for transfers between devices: 249 us -> 104 us
    all_to_all x4 -> x0, starting transfers between devices: 31 us -> none  [the longest x1 8.59 us: per_device(): lax.all_to_all(out_labels, 'wide', split_axis=0, concat_axis=0, tiled=True)]
    scatter x2 -> x0, local copies, waits for them, and re-layouts: 24.1 us -> none  [the longest x1 18 us: per_device(): outgoing = jnp.zeros((device_total * capacity, feature_width), jnp.bfloat...]
    all_to_all x4 -> x0, local copies, waits for them, and re-layouts: 17.6 us -> none  [the longest x1 10.9 us: per_device(): lax.all_to_all(outgoing, 'wide', split_axis=0, concat_axis=0, tiled=True)]
  transfers between devices with their start and end apart: 8 -> 4, of which waited for: 5 -> 4; matrix products, arithmetic and copies ran while one was open for 4% -> 0% of each run, Pallas kernels for 0% -> 26%
where the time goes in v1:
time: 673 us; the launch traced here: 670 us
  waiting for transfers between devices  277 us (41%)
  Pallas kernels  174 us (26%)
  blocking collectives  173 us (26%)
  between operations  14.5 us (2%)
  local copies, waits for them, and re-layouts  13.9 us (2%)
  matrix products  11 us (2%)
    pallas_call x1, Pallas kernels, exchange(): pl.pallas_call(exchange_kernel, out_shape=(jax.ShapeDtypeStruct((clusters...  174 us
    unnamed x5, waiting for transfers between devices  104 us
    unnamed x2, blocking collectives  93.3 us
    reduce_scatter x1, waiting for transfers between devices, per_device(): lax.psum_scatter(partial_value, 'narrow', scatter_dimension=0, tiled=True)  75.5 us
    psum x1, blocking collectives, per_device(): sums_three, weight_three = lax.psum((partial_value, masses), 'wide')  66.3 us
    psum x1, waiting for transfers between devices, per_device(): sums_four, mass_four = lax.psum((sums_four, mass_four), 'narrow')  61.1 us
    psum x1, waiting for transfers between devices, per_device(): sums_three, weight_three = lax.psum((partial_value, masses), 'wide')  36.3 us
    psum x1, blocking collectives, per_device(): sums_four, mass_four = lax.psum((sums_four, mass_four), 'narrow')  13.7 us
  transfers between devices with their start and end apart: 4, of which 4 were waited for; matrix products, arithmetic and copies ran while one was open for 0% of the time, Pallas kernels for 26%

profile of v1, /device:TPU:1, one launch (start us, length us, event | category | flops | bytes accessed | tf_op | source)
XLA Modules:
  0.0 669.9 jit_solution(13491169113794494989)
XLA Ops:
  7.2 0.0 all-reduce.11.cloned.1.call-start
  7.2 0.8 bitcast_dynamic-update-slice_fusion
  8.0 81.4 %all-reduce = s32[512]{0:T(512)S(1)} all-reduce(s32[512]{0:T(512)S(1)} %bitcast_dynamic-update-slice_fusion), channel_id=2, replica_groups=mesh['wide'=32,'narrow'=8] {'wide','narrow'}, use_global_device_ids=true, to_apply=%add | all-reduce | flops 512 | bytes 4096
  89.4 7.2 %gather_fusion = bf16[512,1536]{1,0:T(8,128)(2,1)S(1)} fusion(bf16[2048,1536]{1,0:T(8,128)(2,1)} %emb.1, s32[1024]{0:T(1024)S(1)} %pad_clamp_fusion), kind=kCustom, calls=%fused_computation | custom fusion | bytes 3147776 | tf_op jit(solution)/shard_map/gather | solution.py:309
  96.6 2.0 convert_select_fusion
  98.6 0.0 all-reduce.11.cloned.1.call-update
  98.6 0.0 reduce-scatter.2.cloned.1.call-start
  98.7 0.0 copy-start.4
  98.7 173.8 %shard_map.103 = (f32[256,1536]{1,0:T(8,128)}, f32[8,256]{1,0:T(8,128)}) custom-call(bf16[2048,1536]{1,0:T(8,128)(2,1)} %emb.1, s32[1,2048]{1,0:T(1,128)} %bitcast.15, s32[1,2048]{1,0:T(1,128)} %bitcast.16, s32[1,2048]{1,0:T(1,128)} %bitcast.17), custom_call_target="tpu_custom_call" | custom-call | tf_op jit(solution)/shard_map/pallas_call | solution.py:252
  272.4 0.0 copy-start.2
  272.5 0.7 slice.3
  273.2 0.0 copy-done.4
  273.2 104.0 %all-reduce.11.cloned.1.call-done = f32[512,1536]{1,0:T(8,128)} async-done(((f32[512,1536]{1,0:T(8,128)}), f32[512,1536]{1,0:T(8,128)}) %all-reduce.11.cloned.1.call-update) | async-done | bytes 3145744
  377.1 3.4 scatter_custom_fusion
  380.5 0.0 copy-done.2
  380.5 8.5 %fusion = f32[1024,1536]{1,0:T(8,128)} fusion(f32[256,1536]{1,0:T(8,128)} %scatter_custom_fusion, f32[256]{0:T(256)S(1)} %bitcast.13, s32[256]{0:T(256)S(1)} %copy-done.2), kind=kOutput, calls=%fused_computation.4 | convolution fusion | flops 4832362496 | bytes 7866368 | tf_op jit(solution)/shard_map/dot_general | solution.py:322
  389.0 0.0 copy-start.5
  389.0 0.0 reduce-scatter.2.cloned.1.call-update
  389.0 0.0 copy-start.3
  389.0 0.0 all-reduce.7.cloned.1.call-start
  389.1 75.5 %reduce-scatter.2.cloned.1.call-done = f32[128,1536]{1,0:T(8,128)} async-done(((f32[1024,1536]{1,0:T(8,128)}), f32[128,1536]{1,0:T(8,128)}) %reduce-scatter.2.cloned.1.call-update) | async-done | bytes 786448 | tf_op jit(solution)/shard_map/reduce_scatter | solution.py:330
  464.6 0.0 all-reduce.7.cloned.1.call-update
  464.6 0.0 all-reduce.9.cloned.1.call-start
  464.7 0.0 copy-done.5
  464.7 0.6 dynamic-slice.1
  465.9 0.2 select_reduce_fusion
  466.1 11.9 %all-reduce.2 = f32[1024]{0:T(1024)S(1)} all-reduce(f32[1024]{0:T(1024)S(1)} %select_reduce_fusion), channel_id=5, replica_groups=mesh['wide'=32,'narrow'=8] {'narrow'}, use_global_device_ids=true, to_apply=%region_5.6.clone | all-reduce | flops 1024 | bytes 8192
  478.1 0.1 dynamic-slice.2
  478.1 66.3 %psum.29 = f32[128]{0:T(128)S(1)} all-reduce(f32[128]{0:T(128)S(1)} %dynamic-slice.2), channel_id=1, replica_groups=mesh['wide'=32,'narrow'=8] {'wide'}, use_global_device_ids=true, to_apply=%region_6.7 | all-reduce | flops 128 | bytes 1024 | tf_op jit(solution)/shard_map/psum | solution.py:333
  544.4 36.3 %all-reduce.7.cloned.1.call-done = f32[128,1536]{1,0:T(8,128)} async-done(((f32[128,1536]{1,0:T(8,128)}), f32[128,1536]{1,0:T(8,128)}) %all-reduce.7.cloned.1.call-update) | async-done | bytes 786448 | tf_op jit(solution)/shard_map/psum | solution.py:333
  580.7 1.3 broadcast_divide_fusion.1
  581.9 0.0 copy-done.3
  582.0 0.0 copy-start.1
  582.0 2.6 fusion.5
  584.5 0.0 all-reduce.9.cloned.1.call-update
  584.6 0.0 copy-done.1
  584.6 0.1 select_reduce_fusion.1
  584.7 13.7 %psum.31 = f32[256]{0:T(256)S(1)} all-reduce(f32[256]{0:T(256)S(1)} %select_reduce_fusion.1), channel_id=1, replica_groups=mesh['wide'=32,'narrow'=8] {'narrow'}, use_global_device_ids=true, to_apply=%region_9.10 | all-reduce | flops 256 | bytes 2048 | tf_op jit(solution)/shard_map/psum | solution.py:347
  598.4 0.0 copy-start
  598.4 61.1 %all-reduce.9.cloned.1.call-done = f32[256,1536]{1,0:T(8,128)} async-done(((f32[256,1536]{1,0:T(8,128)}), f32[256,1536]{1,0:T(8,128)}) %all-reduce.9.cloned.1.call-update) | async-done | bytes 1572880 | tf_op jit(solution)/shard_map/psum | solution.py:347
  659.4 2.8 broadcast_divide_fusion
  662.2 0.0 copy-done
  662.2 1.1 copy.17
  (7 shorter events, 0.0 us)
Async XLA Ops:
  7.2 370.0 %all-reduce.11.cloned.1.call-start = ((), (), s32[]{:S(2)}) async-start(), calls=%async_computation.4 | async-start | bytes 6291456
  98.6 366.0 %reduce-scatter.2.cloned.1.call-start = ((), (), s32[]{:S(2)}) async-start(), calls=%async_computation.1 | async-start | bytes 7077888 | tf_op jit(solution)/shard_map/reduce_scatter | solution.py:330
  98.7 174.5 %copy-start.4 = (s32[1,2]{1,0:T(1,128)S(1)}, s32[1,2]{1,0:T(1,128)}, u32[]{:S(2)}) copy-start(s32[1,2]{1,0:T(1,128)} %param.12) | copy-start | bytes 28
  272.4 108.1 %copy-start.2 = (s32[256]{0:T(256)S(1)}, s32[256]{0:T(256)}, u32[]{:S(2)}) copy-start(s32[256]{0:T(256)} %param.14) | copy-start | bytes 3076
  389.0 75.7 %copy-start.5 = (u32[256]{0:T(256)S(1)}, u32[256]{0:T(256)}, u32[]{:S(2)}) copy-start(u32[256]{0:T(256)} %constant.38) | copy-start | bytes 3076
  389.0 192.9 %copy-start.3 = (s32[128]{0:T(128)S(1)}, s32[128]{0:T(128)}, u32[]{:S(2)}) copy-start(s32[128]{0:T(128)} %param.15) | copy-start | bytes 1540
  389.0 191.6 %all-reduce.7.cloned.1.call-start = ((), (), s32[]{:S(2)}) async-start(), calls=%async_computation.2 | async-start | bytes 1572864 | tf_op jit(solution)/shard_map/psum | solution.py:333
  464.6 194.8 %all-reduce.9.cloned.1.call-start = ((), (), s32[]{:S(2)}) async-start(), calls=%async_computation.3 | async-start | bytes 3145728 | tf_op jit(solution)/shard_map/psum | solution.py:347
  582.0 2.6 copy-start.1
  598.4 63.8 %copy-start = (f32[256,1536]{1,0:T(8,128)S(1)}, f32[256,1536]{1,0:T(8,128)}, u32[]{:S(2)}) copy-start(f32[256,1536]{1,0:T(8,128)} %scatter_custom_fusion) | copy-start | bytes 4718596
Sparse Core Ops, SparseCore 0:
  98.7 278.3 all-reduce.10
  389.1 75.4 reduce-scatter.1
  468.2 112.4 all-reduce.6
  584.7 74.7 all-reduce.8

commit v2 on v1

v2 whole, which is shorter than its diff:
```python
import jax
import jax.numpy as jnp
from jax import lax
from jax.experimental import pallas as pl
from jax.experimental.pallas import tpu as pltpu
from jax.sharding import PartitionSpec as P

L4 = 256
CAP = 16
NX, NY, NC, NZ = 4, 4, 2, 8
NW = NX * NY * NC
MESH = pl.DeviceIdType.MESH
SEND_BUFFERS = 2

XY_ORDER = [
    (1, 0), (0, 1), (3, 0), (0, 3), (2, 2), (1, 1), (3, 3), (1, 3),
    (3, 1), (2, 0), (0, 2), (2, 1), (1, 2), (2, 3), (3, 2),
]
WIDE_ORDER = [(dx, dy, dc) for dc in range(NC) for dx, dy in XY_ORDER] + [(0, 0, 1)]


def nt_dot(a, b):
    return lax.dot_general(
        a, b, (((1,), (1,)), ((), ())), preferred_element_type=jnp.float32
    )


def iota(shape, axis):
    return lax.broadcasted_iota(jnp.int32, shape, axis)


def centroid_kernel(
    emb, own, slot, cnt, par2, par3, reseed, donor,
    out2, out3, out4,
    sbuf, rbuf, onehot, pos, lab_send, lab_recv, lab_t, ring_f, ring_b, w_send, w_recv,
    info_z, info_w, tab, req, red_z, red_w, totals, picked,
    part, core_send, core_recv, ring3, ring_d, rows_d, send_d, recv_d, final_d,
    recv_xy, recv_three, three, recv_four, recv_out, acc_four,
    s_sem, r_sem, f_send, f_recv, b_send, b_recv, once, core_s, core_r, s3_sem, r3_sem,
    sd_sem, rd_sem,
):
    rows, width = emb.shape
    half = width // 2
    clusters = out2.shape[0]
    per_z = out3.shape[0]
    mine = per_z // NC
    w = lax.axis_index("wide")
    z = lax.axis_index("narrow")
    x, y, c = w // 8, (w // 2) % 4, w % 2

    def wide_index(d):
        return ((x + d[0]) % NX) * 8 + ((y + d[1]) % NY) * 2 + (c + d[2]) % NC

    def wide_peer(d):
        return (wide_index(d), z)

    def offset(k):
        return k // 8, (k // 2) % 4, k % 2

    def source_of(k):
        dx, dy, dc = offset(k)
        return wide_index((NX - dx, NY - dy, dc))

    def z_peer(k):
        return (w, (z + k) % NZ)

    barrier = pltpu.get_barrier_semaphore()
    for d in WIDE_ORDER:
        pl.semaphore_signal(barrier, inc=1, device_id=wide_peer(d), device_id_type=MESH)
    for k in range(1, NZ):
        pl.semaphore_signal(barrier, inc=1, device_id=z_peer(k), device_id_type=MESH)

    def spread(src, dst, sems, device):
        return pltpu.make_async_remote_copy(
            src_ref=src, dst_ref=dst, send_sem=sems.at[0], recv_sem=sems.at[1],
            device_id=device, device_id_type=MESH,
        )

    def spread_z(src, dst, sems):
        for k in range(1, NZ):
            spread(src, dst.at[k], sems, z_peer(k)).start()

    def join_z(dst, sems):
        at = pl.ds(1, NZ - 1)
        spread(dst.at[at], dst.at[at], sems, z_peer(1)).wait()

    def spread_wide(src, dst, sems):
        for d in WIDE_ORDER:
            k = d[0] * 8 + d[1] * 2 + d[2]
            spread(src, dst.at[k], sems, wide_peer(d)).start()

    def join_wide(dst, sems):
        at = pl.ds(1, NW - 1)
        spread(dst.at[at], dst.at[at], sems, wide_peer((0, 0, 1))).wait()

    sem_info_z, sem_info_w, sem_lab, sem_w = once.at[0], once.at[1], once.at[2], once.at[3]
    sem_red_z, sem_red_w, sem_xy, sem_d = once.at[4], once.at[5], once.at[6], once.at[7]
    sem_three, sem_four, sem_out = once.at[8], once.at[9], once.at[10]

    slots = iota((1, clusters), 1)
    parent = par2[...].astype(jnp.float32)
    hits = [slots == reseed[0:1, k : k + 1] for k in range(2)]
    grands = [jnp.sum(jnp.where(h, parent, 0.0), axis=1, keepdims=True) for h in hits]
    table = parent + jnp.where(hits[0] | hits[1], 1024.0, 0.0)
    lane = iota((1, 128), 1)
    extra = jnp.zeros((1, 128), jnp.float32)
    for i, v in enumerate(
        [donor[0:1, 0:1], donor[0:1, 1:2], grands[0], grands[1], reseed[0:1, 0:1], reseed[0:1, 1:2]]
    ):
        extra = jnp.where(lane == i, v.astype(jnp.float32), extra)
    info_z[0, :, 0:clusters] = jnp.where(iota((NZ, clusters), 0) == z, table, 0.0)
    info_z[0, :, clusters : clusters + 128] = jnp.where(iota((NZ, 128), 0) == z, extra, 0.0)

    owner = own[...]
    target = owner // NZ
    rel = (
        ((target // 8 - x) & 3) * 8 + (((target // 2) - y) & 3) * 2 + ((target - c) & 1)
    )
    step = 256
    upper = (iota((step, step), 0) < iota((step, step), 1)).astype(jnp.bfloat16)
    carry = jnp.zeros((step, 1), jnp.float32)
    for b in range(rows // step):
        cols = slice(b * step, (b + 1) * step)
        hit = iota((step, step), 0) == owner[:, cols]
        mark = hit.astype(jnp.bfloat16)
        earlier = jnp.dot(mark, upper, preferred_element_type=jnp.float32) + carry
        mark32 = hit.astype(jnp.float32)
        rank = jnp.sum(earlier * mark32, axis=0, keepdims=True)
        carry = carry + jnp.sum(mark32, axis=1, keepdims=True)
        pos[0:1, cols] = rel[:, cols] * CAP + rank.astype(jnp.int32)
    pos[1:2, :] = owner % NZ

    pl.semaphore_wait(barrier, NW - 1 + NZ - 1)
    spread_z(info_z.at[0], info_z, sem_info_z)

    places = NW * CAP
    tile = 256

    def fill_onehot(where_row):
        for i in range(places // tile):
            ids = iota((tile, rows), 0) + i * tile
            onehot[i * tile : (i + 1) * tile, :] = (ids == where_row).astype(jnp.bfloat16)

    fill_onehot(pos[0:1, :])
    deep = iota((128, rows), 0)
    z_of = pos[1:2, :]
    labels = jnp.where(
        deep == 2 * z_of, slot[...], jnp.where(deep == 2 * z_of + 1, cnt[...], 0)
    ).astype(jnp.float32).astype(jnp.bfloat16)
    lab_send[...] = nt_dot(onehot[...], labels).astype(jnp.bfloat16)
    lab_recv[0:CAP, :] = lab_send[0:CAP, :]

    def send_wide(src, dst, sem_s, sem_r):
        for d in WIDE_ORDER:
            k = d[0] * 8 + d[1] * 2 + d[2]
            at = pl.ds(k * CAP, CAP)
            pltpu.make_async_remote_copy(
                src_ref=src.at[at], dst_ref=dst.at[at], send_sem=sem_s, recv_sem=sem_r,
                device_id=wide_peer(d), device_id_type=MESH,
            ).start()

    def all_wide(src, dst, sem_s, sem_r):
        at = pl.ds(CAP, places - CAP)
        return pltpu.make_async_remote_copy(
            src_ref=src.at[at], dst_ref=dst.at[at], send_sem=sem_s, recv_sem=sem_r,
            device_id=wide_peer((0, 0, 1)), device_id_type=MESH,
        )

    send_wide(lab_send, lab_recv, sem_lab.at[0], sem_lab.at[1])

    def block_f(t):
        return (z + 2 * NZ - 1 - t) % NZ

    def block_b(t):
        return (z + 1 + t) % NZ

    def pack(t):
        b = lax.rem(t, SEND_BUFFERS)

        @pl.when(t >= SEND_BUFFERS)
        def _():
            all_wide(sbuf.at[b], rbuf.at[t], s_sem.at[b], r_sem.at[t]).wait_send()

        for h, blk in enumerate((block_f(t), block_b(t))):
            fill_onehot(jnp.where(pos[1:2, :] == blk, pos[0:1, :], -1))

            def column(n, _, h=h):
                at = pl.ds(pl.multiple_of(h * half + n * tile, tile), tile)
                sbuf[b, :, at] = jnp.dot(
                    onehot[...], emb[:, at], preferred_element_type=jnp.float32
                ).astype(jnp.bfloat16)
                return 0

            lax.fori_loop(0, half // tile, column, 0)
        rbuf[t, 0:CAP, :] = sbuf[b, 0:CAP, :]

    def send(t):
        b = lax.rem(t, SEND_BUFFERS)
        send_wide(sbuf.at[b], rbuf.at[t], s_sem.at[b], r_sem.at[t])

    join_z(info_z, sem_info_z)
    whole = info_z[0]
    for k in range(1, NZ):
        whole = whole + info_z[k]
    info_w[0] = whole
    spread_wide(info_w.at[0], info_w, sem_info_w)
    pack(0)
    send(0)

    all_wide(lab_send, lab_recv, sem_lab.at[0], sem_lab.at[1]).wait()
    eye = (iota((16, 128), 0) == iota((16, 128), 1)).astype(jnp.bfloat16)
    lab_t[...] = nt_dot(eye, lab_recv[...])

    def matched(blk):
        ids = iota((clusters, places), 0).astype(jnp.float32)
        return ids == lab_t[pl.ds(2 * blk, 1), :], lab_t[pl.ds(2 * blk + 1, 1), :]

    def weigh(k, _):
        hit, counts = matched((z + k) % NZ)
        counts = jnp.broadcast_to(counts, (8, places)).astype(jnp.bfloat16)
        w_send[k] = nt_dot(counts, hit.astype(jnp.float32).astype(jnp.bfloat16))
        return 0

    lax.fori_loop(0, NZ, weigh, 0)
    for k in range(1, NZ):
        spread(w_send.at[k], w_recv.at[k], sem_w, z_peer(k)).start()

    join_wide(info_w, sem_info_w)

    def arrange(k, _):
        src = source_of(k)
        tab[pl.ds(pl.multiple_of(src * NZ, NZ), NZ), :] = info_w[k, :, 0:clusters]
        for zz in range(NZ):
            req[pl.ds(zz * NW + src, 1), :] = info_w[k, zz : zz + 1, clusters : clusters + 128]
        return 0

    lax.fori_loop(0, NW, arrange, 0)
    across = jnp.transpose(tab[...])
    high = jnp.floor(across * (1.0 / 64.0))
    low = (across - 64.0 * high).astype(jnp.bfloat16)
    high = high.astype(jnp.bfloat16)
    for b in range(rows // step):
        cols = slice(b * step, (b + 1) * step)
        mark = (iota((step, step), 0) == own[:, cols]).astype(jnp.bfloat16)
        values = 64.0 * jnp.dot(high, mark, preferred_element_type=jnp.float32) + jnp.dot(
            low, mark, preferred_element_type=jnp.float32
        )
        found = jnp.sum(
            jnp.where(iota((clusters, step), 0) == slot[:, cols], values, 0.0),
            axis=0, keepdims=True,
        ).astype(jnp.int32)
        gone = found >= 1024
        true_parent = jnp.where(gone, found - 1024, found)
        pos[2:3, cols] = jnp.where(gone, -1, true_parent)
        pos[3:4, cols] = true_parent

    devices = NW * NZ
    place = iota((devices, 1), 0)
    owner_of = (place % NW) * NZ + place // NW
    ident = own[...] * clusters + slot[...]
    for k in range(2):
        asked = owner_of * clusters + req[:, 4 + k : 5 + k].astype(jnp.int32)
        onehot[k * devices : (k + 1) * devices, :] = (asked == ident).astype(jnp.bfloat16)
    counts32 = cnt[...].astype(jnp.float32)
    counts8 = jnp.broadcast_to(counts32, (8, rows)).astype(jnp.bfloat16)
    true_parent = pos[3:4, :]
    by_z = jnp.where(iota((8, rows), 0) == true_parent // per_z, counts32, 0.0).astype(jnp.bfloat16)
    inside = (iota((per_z, rows), 0) == true_parent % per_z).astype(jnp.bfloat16)
    red_z[0, :, 0 : 2 * devices] = nt_dot(counts8, onehot[...])
    red_z[0, :, 2 * devices : 2 * devices + per_z] = nt_dot(by_z, inside)
    spread_z(red_z.at[0], red_z, sem_red_z)

    def reduce_weights_z():
        join_z(red_z, sem_red_z)
        total = red_z[0]
        for k in range(1, NZ):
            total = total + red_z[k]
        red_w[0] = total
        spread_wide(red_w.at[0], red_w, sem_red_w)

    def reduce_weights_wide():
        join_wide(red_w, sem_red_w)
        total = red_w[0].astype(jnp.int32)
        for k in range(1, NW):
            total = total + red_w[k].astype(jnp.int32)
        totals[...] = total.astype(jnp.float32)

    def pick_donors():
        first = (w * NZ + z) * rows
        for k in range(2):
            local = req[:, k : k + 1].astype(jnp.int32) - first
            onehot[k * devices : (k + 1) * devices, :] = (
                iota((devices, rows), 1) == local
            ).astype(jnp.bfloat16)

        def column(n, _):
            at = pl.ds(pl.multiple_of(n * tile, tile), tile)
            picked[:, at] = jnp.dot(
                onehot[...], emb[:, at], preferred_element_type=jnp.float32
            ).astype(jnp.bfloat16)
            return 0

        lax.fori_loop(0, width // tile, column, 0)

    def core_copy(s):
        b = lax.rem(s, 2)
        return pltpu.make_async_remote_copy(
            src_ref=core_send.at[b], dst_ref=core_recv.at[s],
            send_sem=core_s.at[b], recv_sem=core_r.at[s],
            device_id=wide_peer((0, 0, 1)), device_id_type=MESH,
        )

    def three_terms(value):
        first = value.astype(jnp.bfloat16)
        rest = value - first.astype(jnp.float32)
        second = rest.astype(jnp.bfloat16)
        return first, second, (rest - second.astype(jnp.float32)).astype(jnp.bfloat16)

    def local_three(s):
        b = lax.rem(s, 2)

        @pl.when(s >= 2)
        def _():
            core_copy(s - 2).wait_send()

        grand_rows = jnp.transpose(req[...])
        for h, blk in enumerate((block_f(s), block_b(s))):
            base = jnp.where(
                iota((per_z, rows), 0) + per_z * blk == pos[2:3, :], cnt[...], 0
            ).astype(jnp.float32).astype(jnp.bfloat16)
            ids = (iota((per_z, devices), 0) + per_z * blk).astype(jnp.float32)
            heavy = [
                three_terms(
                    jnp.where(
                        ids == grand_rows[2 + k : 3 + k, :],
                        totals[0:1, k * devices : (k + 1) * devices],
                        0.0,
                    )
                )
                for k in range(2)
            ]
            for n in range(half // tile):
                at = slice(h * half + n * tile, h * half + (n + 1) * tile)
                value = jnp.dot(base, emb[:, at], preferred_element_type=jnp.float32)
                for k in range(2):
                    for term in heavy[k]:
                        value = value + jnp.dot(
                            term,
                            picked[k * devices : (k + 1) * devices, at],
                            preferred_element_type=jnp.float32,
                        )
                part[b, h, :, n * tile : (n + 1) * tile] = value
            core_send[b, h] = part[b, h, pl.ds(pl.multiple_of((1 - c) * mine, mine), mine), :]
        core_copy(s).start()

    def ring3_copy(h, s):
        return pltpu.make_async_remote_copy(
            src_ref=ring3.at[h, s], dst_ref=ring3.at[h, s + 1],
            send_sem=s3_sem.at[h, s], recv_sem=r3_sem.at[h, s + 1],
            device_id=z_peer((1, NZ - 1)[h]), device_id_type=MESH,
        )

    def ring_d_copy(h, s):
        return pltpu.make_async_remote_copy(
            src_ref=ring_d.at[h, s], dst_ref=ring_d.at[h, s + 1],
            send_sem=sd_sem.at[h, s], recv_sem=rd_sem.at[h, s + 1],
            device_id=z_peer((1, NZ - 1)[h]), device_id_type=MESH,
        )

    def step_three(s):
        @pl.when(s < NZ - 1)
        def _():
            local_three(s + 1)

        b = lax.rem(s, 2)
        core_copy(s).wait_recv()
        for h, blk in enumerate((block_f(s), block_b(s))):
            at = pl.ds(pl.multiple_of(c * mine, mine), mine)
            value = part[b, h, at, :] + core_recv[s, h]
            chosen = picked[pl.ds(pl.multiple_of(h * devices + blk * NW, NW), NW), :]

            @pl.when(s == 0)
            def _(h=h, value=value, chosen=chosen):
                ring3[h, s] = value
                ring_d[h, s] = chosen

            @pl.when(s > 0)
            def _(h=h, value=value, chosen=chosen):
                ring3_copy(h, s - 1).wait_recv()
                ring3[h, s] += value
                ring_d_copy(h, s - 1).wait_recv()
                ring_d[h, s] = (
                    ring_d[h, s].astype(jnp.float32) + chosen.astype(jnp.float32)
                ).astype(jnp.bfloat16)

            @pl.when(s < NZ - 1)
            def _(h=h):
                ring3_copy(h, s).start()
                ring_d_copy(h, s).start()

    quarter = width // 4

    def piece(xx, yy):
        i = xx * NY + yy
        return ring3.at[i // 8, NZ - 1, pl.ds(pl.multiple_of((i % 8) * 8, 8), 8)]

    def send_three_and_donors():
        recv_xy[0] = piece(x, y)[...]
        for dx, dy in XY_ORDER:
            spread(
                piece((x + dx) % NX, (y + dy) % NY), recv_xy.at[dx * NY + dy], sem_xy,
                wide_peer((dx, dy, 0)),
            ).start()
        for h in range(2):
            rows_d[h] = ring_d[h, NZ - 1].astype(jnp.float32)

        def lay(k, _):
            to = wide_index(offset(k))
            for h in range(2):
                for j in range(4):
                    send_d[k, 4 * h + j : 4 * h + j + 1, :] = rows_d[
                        h, pl.ds(to, 1), j * quarter : (j + 1) * quarter
                    ]
            return 0

        lax.fori_loop(0, NW, lay, 0)
        recv_d[0] = send_d[0]
        for d in WIDE_ORDER:
            k = d[0] * 8 + d[1] * 2 + d[2]
            spread(send_d.at[k], recv_d.at[k], sem_d, wide_peer(d)).start()

    def join_three_and_donors():
        at = pl.ds(1, NX * NY - 1)
        spread(recv_xy.at[at], recv_xy.at[at], sem_xy, wide_peer((0, 1, 0))).wait()
        total = recv_xy[0]
        for k in range(1, NX * NY):
            total = total + recv_xy[k]
        recv_three[0] = total
        join_wide(recv_d, sem_d)
        total = recv_d[0]
        for k in range(1, NW):
            total = total + recv_d[k]
        final_d[...] = total

    def finish_three():
        join_wide(recv_three, sem_three)

        def lay(k, _):
            src = source_of(k)
            i = src // 2
            row = (src % 2) * mine + (i % 8) * 8
            three[i // 8, pl.ds(pl.multiple_of(row, 8), 8), :] = recv_three[k]
            return 0

        lax.fori_loop(0, NW, lay, 0)
        masses = totals[:, 2 * devices : 2 * devices + per_z]
        mass_row = jnp.sum(
            jnp.where(iota((8, per_z), 0) == z, masses, 0.0), axis=0, keepdims=True
        )
        diagonal = iota((per_z, per_z), 0) == iota((per_z, per_z), 1)
        mass = jnp.sum(jnp.where(diagonal, mass_row, 0.0), axis=1, keepdims=True)
        mass = jnp.maximum(mass, 1.0)
        chosen = par3[...] == iota((8, per_z), 0) + 8 * w
        pick = chosen.astype(jnp.float32).astype(jnp.bfloat16)
        for h in range(2):
            out3[:, h * half : (h + 1) * half] = three[h] / mass
            total = jnp.zeros((8, half), jnp.float32)
            for term in three_terms(three[h]):
                total = total + jnp.dot(pick, term, preferred_element_type=jnp.float32)
            recv_four[0, :, h * half : (h + 1) * half] = total
        mass_four = jnp.sum(jnp.where(chosen, mass_row, 0.0), axis=1, keepdims=True)
        recv_four[0, :, width : width + 128] = jnp.broadcast_to(mass_four, (8, 128))
        spread_z(recv_four.at[0], recv_four, sem_four)

    def send_four():
        join_z(recv_four, sem_four)
        acc_four[...] = recv_four[z]
        for zz in range(1, NZ):
            acc_four[...] += recv_four[(z + NZ - zz) % NZ]
        mass = jnp.maximum(acc_four[:, width : width + 1], 1.0)
        recv_out[0] = acc_four[:, 0:width] / mass
        spread_wide(recv_out.at[0], recv_out, sem_out)

    def finish_four():
        join_wide(recv_out, sem_out)

        def lay(k, _):
            out4[pl.ds(pl.multiple_of(source_of(k) * 8, 8), 8), :] = recv_out[k]
            return 0

        lax.fori_loop(0, NW, lay, 0)

    def ring_copy(ring, t, sems, k):
        return pltpu.make_async_remote_copy(
            src_ref=ring.at[t], dst_ref=ring.at[t + 1],
            send_sem=sems[0].at[t], recv_sem=sems[1].at[t + 1],
            device_id=z_peer(k), device_id_type=MESH,
        )

    rings = (
        (ring_f, (f_send, f_recv), 1, block_f),
        (ring_b, (b_send, b_recv), NZ - 1, block_b),
    )

    def reduce_stage(t):
        all_wide(sbuf.at[0], rbuf.at[t], s_sem.at[0], r_sem.at[t]).wait_recv()
        for h, (ring, sems, k, block) in enumerate(rings):
            hit, counts = matched(block(t))
            assign = jnp.where(hit, counts, 0.0).astype(jnp.bfloat16)

            @pl.when(t > 0)
            def _(ring=ring, sems=sems, k=k):
                ring_copy(ring, t - 1, sems, k).wait_recv()

            for n in range(half // tile):
                at = slice(n * tile, (n + 1) * tile)
                value = jnp.dot(
                    assign,
                    rbuf[t, :, h * half + n * tile : h * half + (n + 1) * tile],
                    preferred_element_type=jnp.float32,
                )

                @pl.when(t == 0)
                def _(ring=ring, at=at, value=value):
                    ring[t, :, at] = value

                @pl.when(t > 0)
                def _(ring=ring, at=at, value=value):
                    ring[t, :, at] += value

            @pl.when(t < NZ - 1)
            def _(ring=ring, sems=sems, k=k):
                ring_copy(ring, t, sems, k).start()

    def at_stage(t, which, work):
        pl.when(t == which)(work)

    def stage(t, _):
        @pl.when(t < NZ - 1)
        def _():
            pack(t + 1)

        at_stage(t, 0, reduce_weights_z)

        @pl.when((t >= 1) & (t <= 4))
        def _():
            step_three(2 * t - 2)

        at_stage(t, 5, send_three_and_donors)
        at_stage(t, 6, lambda: spread_wide(recv_three.at[0], recv_three, sem_three))
        at_stage(t, 7, send_four)

        @pl.when(t < NZ - 1)
        def _():
            send(t + 1)

        reduce_stage(t)

        @pl.when(t == 0)
        def _():
            reduce_weights_wide()
            pick_donors()
            local_three(0)

        @pl.when((t >= 1) & (t <= 4))
        def _():
            step_three(2 * t - 1)

        at_stage(t, 5, join_three_and_donors)
        at_stage(t, 6, finish_three)
        return 0

    lax.fori_loop(0, NZ, stage, 0)

    others = pl.ds(1, NZ - 1)
    spread(w_send.at[others], w_recv.at[others], sem_w, z_peer(1)).wait()
    total = w_send[0]
    for k in range(1, NZ):
        total = total + w_recv[k]
    diagonal = iota((clusters, clusters), 0) == iota((clusters, clusters), 1)
    mass = jnp.sum(jnp.where(diagonal, total[0:1, :], 0.0), axis=1, keepdims=True)
    mass = jnp.maximum(mass, 1.0)
    seeded = [iota((clusters, 1), 0) == reseed[0:1, k : k + 1] for k in range(2)]
    for j in range(4):
        ring = rings[j // 2][0]
        at = (j % 2) * quarter
        value = ring[NZ - 1, :, at : at + quarter] / mass
        for k in range(2):
            value = jnp.where(seeded[k], final_d[4 * k + j : 4 * k + j + 1, :], value)
        out2[:, j * quarter : (j + 1) * quarter] = value

    finish_four()
    for b in range(SEND_BUFFERS):
        all_wide(sbuf.at[b], rbuf.at[0], s_sem.at[b], r_sem.at[0]).wait_send()
    for b in range(2):
        core_copy(b).wait_send()

    def drain(t, _):
        for h, (ring, sems, k, block) in enumerate(rings):
            ring_copy(ring, t, sems, k).wait_send()
            ring3_copy(h, t).wait_send()
            ring_d_copy(h, t).wait_send()
        return 0

    lax.fori_loop(0, NZ - 1, drain, 0)


def per_device(
    embeddings,
    point_counts,
    owner_ids,
    owner_slots,
    reseed_slots,
    donor_ids,
    parents_two,
    parents_three,
):
    rows, width = embeddings.shape
    clusters = parents_two.shape[0]
    per_z = parents_three.shape[0]
    half = width // 2
    places = NW * CAP
    devices = NW * NZ
    f32, bf16 = jnp.float32, jnp.bfloat16
    vmem = pl.BlockSpec(memory_space=pltpu.VMEM)
    dma = pltpu.SemaphoreType.DMA
    return pl.pallas_call(
        centroid_kernel,
        out_shape=(
            jax.ShapeDtypeStruct((clusters, width), f32),
            jax.ShapeDtypeStruct((per_z, width), f32),
            jax.ShapeDtypeStruct((L4, width), f32),
        ),
        in_specs=[vmem] * 8,
        out_specs=(vmem,) * 3,
        scratch_shapes=[
            pltpu.VMEM((SEND_BUFFERS, places, width), bf16),
            pltpu.VMEM((NZ, places, width), bf16),
            pltpu.VMEM((places, rows), bf16),
            pltpu.VMEM((8, rows), jnp.int32),
            pltpu.VMEM((places, 128), bf16),
            pltpu.VMEM((places, 128), bf16),
            pltpu.VMEM((16, places), f32),
            pltpu.VMEM((NZ, clusters, half), f32),
            pltpu.VMEM((NZ, clusters, half), f32),
            pltpu.VMEM((NZ, 8, clusters), f32),
            pltpu.VMEM((NZ, 8, clusters), f32),
            pltpu.VMEM((NZ, NZ, clusters + 128), f32),
            pltpu.VMEM((NW, NZ, clusters + 128), f32),
            pltpu.VMEM((devices, clusters), f32),
            pltpu.VMEM((devices, 128), f32),
            pltpu.VMEM((NZ, 8, 2 * devices + per_z), f32),
            pltpu.VMEM((NW, 8, 2 * devices + per_z), f32),
            pltpu.VMEM((8, 2 * devices + per_z), f32),
            pltpu.VMEM((2 * devices, width), bf16),
            pltpu.VMEM((2, 2, per_z, half), f32),
            pltpu.VMEM((2, 2, per_z // NC, half), f32),
            pltpu.VMEM((NZ, 2, per_z // NC, half), f32),
            pltpu.VMEM((2, NZ, per_z // NC, half), f32),
            pltpu.VMEM((2, NZ, NW, width), bf16),
            pltpu.VMEM((2, NW, width), f32),
            pltpu.VMEM((NW, 8, width // 4), f32),
            pltpu.VMEM((NW, 8, width // 4), f32),
            pltpu.VMEM((8, width // 4), f32),
            pltpu.VMEM((NX * NY, 8, half), f32),
            pltpu.VMEM((NW, 8, half), f32),
            pltpu.VMEM((2, per_z, half), f32),
            pltpu.VMEM((NZ, 8, width + 128), f32),
            pltpu.VMEM((NW, 8, width), f32),
            pltpu.VMEM((8, width + 128), f32),
            dma((SEND_BUFFERS,)),
            dma((NZ,)),
            dma((NZ,)),
            dma((NZ,)),
            dma((NZ,)),
            dma((NZ,)),
            dma((11, 2)),
            dma((2,)),
            dma((NZ,)),
            dma((2, NZ)),
            dma((2, NZ)),
            dma((2, NZ)),
            dma((2, NZ)),
        ],
        compiler_params=pltpu.CompilerParams(
            collective_id=0, has_side_effects=True, vmem_limit_bytes=63 * 2**20
        ),
    )(
        embeddings,
        owner_ids.reshape(1, rows),
        owner_slots.reshape(1, rows),
        point_counts.reshape(1, rows),
        parents_two.reshape(1, clusters),
        parents_three.reshape(1, per_z),
        reseed_slots,
        donor_ids,
    )


def solution(mesh):
    in_specs = (
        P(("wide", "narrow"), None),
        P(("wide", "narrow")),
        P(("wide", "narrow"), None),
        P(("wide", "narrow"), None),
        P(("wide", "narrow"), None),
        P(("wide", "narrow"), None),
        P(("wide", "narrow")),
        P("narrow"),
    )
    out_specs = (P(("wide", "narrow"), None), P("narrow", None), P())
    return jax.shard_map(
        per_device, mesh=mesh, in_specs=in_specs, out_specs=out_specs, check_vma=False
    )
```

time: 673 us -> 271 us (0.40)
  waiting for transfers between devices: 277 us -> 0 us
  blocking collectives: 173 us -> 0 us
  Pallas kernels: 174 us -> 261 us
  between operations: 14.5 us -> 0.65 us
  matrix products: 11 us -> 0 us
  local copies, waits for them, and re-layouts: 13.9 us -> 5.57 us
    unnamed x5 -> x0, waiting for transfers between devices: 104 us -> none
    psum x2 -> x0, waiting for transfers between devices: 97.3 us -> none  [the longest x1 61.1 us: per_device(): sums_four, mass_four = lax.psum((sums_four, mass_four), 'narrow')]
    unnamed x2 -> x0, blocking collectives: 93.3 us -> none
    pallas_call x1, Pallas kernels: 174 us -> 261 us  [per_device(): pl.pallas_call(centroid_kernel, out_shape=(jax.ShapeDtypeStruct((clusters...]
    psum x2 -> x0, blocking collectives: 80 us -> none  [the longest x1 66.3 us: per_device(): sums_three, weight_three = lax.psum((partial_value, masses), 'wide')]
    reduce_scatter x1 -> x0, waiting for transfers between devices: 75.5 us -> none  [per_device(): lax.psum_scatter(partial_value, 'narrow', scatter_dimension=0, tiled=True)]
    dot_general x2 -> x0, matrix products: 11 us -> none  [the longest x1 8.47 us: per_device(): jnp.dot(assign_three, centre_two, precision=lax.Precision.HIGHEST, prefer...]
    gather x1 -> x0, local copies, waits for them, and re-layouts: 7.2 us -> none  [per_device(): embeddings[jnp.clip(local_row, 0, rows_local - 1)].astype(jnp.float32)]
  transfers between devices with their start and end apart: 4 -> 0, of which waited for: 4 -> 0; matrix products, arithmetic and copies ran while one was open for 0% -> 0% of each run, Pallas kernels for 26% -> 0%
where the time goes in v2:
time: 271 us; the launch traced here: 267 us
  Pallas kernels  261 us (96%)
  local copies, waits for them, and re-layouts  5.57 us (2%)
    pallas_call x1, Pallas kernels, per_device(): pl.pallas_call(centroid_kernel, out_shape=(jax.ShapeDtypeStruct((clusters...  261 us
    unnamed x7, local copies, waits for them, and re-layouts  5.57 us

profile of v2, /device:TPU:1, one launch (start us, length us, event | category | flops | bytes accessed | tf_op | source)
XLA Modules:
  0.0 267.4 jit_solution(1007756248522436079)
XLA Ops:
  0.6 261.2 %shard_map.103 = (f32[256,1536]{1,0:T(8,128)}, f32[128,1536]{1,0:T(8,128)}, f32[256,1536]{1,0:T(8,128)}) custom-call(bf16[2048,1536]{1,0:T(8,128)(2,1)} %emb.1, s32[1,2048]{1,0:T(1,128)} %bitcast.5, s32[1,2048]{1,0:T(1,128)} %bitcast.6, s32[1,2048]{1,0:T(1,128)} %bitcast.7, s32[1,256]{1,0:T(1,128)} %bitcast.8, s32[1,128]{1,0:T(1,128)} %bitcast.9, ...), custom_call_target="tpu_custom_call" | custom-call | tf_op jit(solution)/shard_map/pallas_call | solution.py:627
  261.8 0.0 copy-start.1
  261.8 2.7 %copy.14 = f32[256,1536]{1,0:T(8,128)} copy(f32[256,1536]{1,0:T(8,128)} %get-tuple-element.6) | data formatting | bytes 3145728
  264.5 0.0 copy-done.1
  264.5 0.0 copy-start
  264.5 0.9 copy.15
  265.4 0.8 copy-done
  266.2 1.1 copy.16
Async XLA Ops:
  261.8 2.7 %copy-start.1 = (f32[128,1536]{1,0:T(8,128)S(1)}, f32[128,1536]{1,0:T(8,128)}, u32[]{:S(2)}) copy-start(f32[128,1536]{1,0:T(8,128)} %get-tuple-element.7) | copy-start | bytes 2359300
  264.5 1.7 copy-start

commit v3 on v2

--- a/solution.py
+++ b/solution.py
@@ -10,7 +10,8 @@
 NX, NY, NC, NZ = 4, 4, 2, 8
 NW = NX * NY * NC
 MESH = pl.DeviceIdType.MESH
-SEND_BUFFERS = 2
+TOP = 32767.0
+SEND_BUFFERS = 3
 
 XY_ORDER = [
     (1, 0), (0, 1), (3, 0), (0, 3), (2, 2), (1, 1), (3, 3), (1, 3),
@@ -19,6 +20,10 @@
 WIDE_ORDER = [(dx, dy, dc) for dc in range(NC) for dx, dy in XY_ORDER] + [(0, 0, 1)]
 
 
+def rel_of(d):
+    return (d[2] * NX + d[0]) * NY + d[1]
+
+
 def nt_dot(a, b):
     return lax.dot_general(
         a, b, (((1,), (1,)), ((), ())), preferred_element_type=jnp.float32
@@ -30,15 +35,17 @@
 
 
 def centroid_kernel(
-    emb, own, slot, cnt, par2, par3, reseed, donor,
+    emb_hbm, own, slot, cnt, par2, par3, reseed, donor,
     out2, out3, out4,
-    sbuf, rbuf, onehot, pos, lab_send, lab_recv, lab_t, ring_f, ring_b, w_send, w_recv,
-    info_z, info_w, tab, req, red_z, red_w, totals, picked,
+    emb, sbuf, rbuf, onehot, pos, lab_send, lab_recv, lab_t, ring_q, ring_s, acc, turn, w_send, w_recv,
+    info_z, info_w, tab, req, red_z, red_w, red_c, totals, picked, donors_c,
     part, core_send, core_recv, ring3, ring_d, rows_d, send_d, recv_d, final_d,
     recv_xy, recv_three, three, recv_four, recv_out, acc_four,
-    s_sem, r_sem, f_send, f_recv, b_send, b_recv, once, core_s, core_r, s3_sem, r3_sem,
+    load_sem, s_sem, r_sem, q_send, q_recv, sc_send, sc_recv, once, core_s, core_r, s3_sem, r3_sem,
     sd_sem, rd_sem,
 ):
+    load = pltpu.make_async_copy(emb_hbm, emb, load_sem.at[0])
+    load.start()
     rows, width = emb.shape
     half = width // 2
     clusters = out2.shape[0]
@@ -55,7 +62,7 @@
         return (wide_index(d), z)
 
     def offset(k):
-        return k // 8, (k // 2) % 4, k % 2
+        return (k // NY) % NX, k % NY, k // (NX * NY)
 
     def source_of(k):
         dx, dy, dc = offset(k)
@@ -84,18 +91,23 @@
         at = pl.ds(1, NZ - 1)
         spread(dst.at[at], dst.at[at], sems, z_peer(1)).wait()
 
-    def spread_wide(src, dst, sems):
-        for d in WIDE_ORDER:
-            k = d[0] * 8 + d[1] * 2 + d[2]
-            spread(src, dst.at[k], sems, wide_peer(d)).start()
-
-    def join_wide(dst, sems):
-        at = pl.ds(1, NW - 1)
-        spread(dst.at[at], dst.at[at], sems, wide_peer((0, 0, 1))).wait()
+    def spread_xy(src, dst, sems):
+        for dx, dy in XY_ORDER:
+            spread(src, dst.at[dx * NY + dy], sems, wide_peer((dx, dy, 0))).start()
+
+    def join_xy(dst, sems):
+        at = pl.ds(1, NX * NY - 1)
+        spread(dst.at[at], dst.at[at], sems, wide_peer((0, 1, 0))).wait()
+
+    def to_core(dst, sems):
+        here, there = pl.ds(0, NX * NY), pl.ds(NX * NY, NX * NY)
+        return spread(dst.at[here], dst.at[there], sems, wide_peer((0, 0, 1)))
 
     sem_info_z, sem_info_w, sem_lab, sem_w = once.at[0], once.at[1], once.at[2], once.at[3]
     sem_red_z, sem_red_w, sem_xy, sem_d = once.at[4], once.at[5], once.at[6], once.at[7]
     sem_three, sem_four, sem_out = once.at[8], once.at[9], once.at[10]
+    sem_info_c, sem_red_c, sem_three_c = once.at[11], once.at[12], once.at[13]
+    sem_out_c, sem_donors_c = once.at[14], once.at[15]
 
     slots = iota((1, clusters), 1)
     parent = par2[...].astype(jnp.float32)
@@ -114,7 +126,7 @@
     owner = own[...]
     target = owner // NZ
     rel = (
-        ((target // 8 - x) & 3) * 8 + (((target // 2) - y) & 3) * 2 + ((target - c) & 1)
+        ((target - c) & 1) * 16 + ((target // 8 - x) & 3) * 4 + (((target // 2) - y) & 3)
     )
     step = 256
     upper = (iota((step, step), 0) < iota((step, step), 1)).astype(jnp.bfloat16)
@@ -152,8 +164,7 @@
 
     def send_wide(src, dst, sem_s, sem_r):
         for d in WIDE_ORDER:
-            k = d[0] * 8 + d[1] * 2 + d[2]
-            at = pl.ds(k * CAP, CAP)
+            at = pl.ds(rel_of(d) * CAP, CAP)
             pltpu.make_async_remote_copy(
                 src_ref=src.at[at], dst_ref=dst.at[at], send_sem=sem_s, recv_sem=sem_r,
                 device_id=wide_peer(d), device_id_type=MESH,
@@ -198,15 +209,19 @@
         b = lax.rem(t, SEND_BUFFERS)
         send_wide(sbuf.at[b], rbuf.at[t], s_sem.at[b], r_sem.at[t])
 
+    load.wait()
+    pack(0)
     join_z(info_z, sem_info_z)
     whole = info_z[0]
     for k in range(1, NZ):
         whole = whole + info_z[k]
     info_w[0] = whole
-    spread_wide(info_w.at[0], info_w, sem_info_w)
-    pack(0)
+    spread_xy(info_w.at[0], info_w, sem_info_w)
     send(0)
 
+    turn[...] = jnp.zeros(turn.shape, jnp.float32)
+    join_xy(info_w, sem_info_w)
+    to_core(info_w, sem_info_c).start()
     all_wide(lab_send, lab_recv, sem_lab.at[0], sem_lab.at[1]).wait()
     eye = (iota((16, 128), 0) == iota((16, 128), 1)).astype(jnp.bfloat16)
     lab_t[...] = nt_dot(eye, lab_recv[...])
@@ -225,13 +240,16 @@
     for k in range(1, NZ):
         spread(w_send.at[k], w_recv.at[k], sem_w, z_peer(k)).start()
 
-    join_wide(info_w, sem_info_w)
+    to_core(info_w, sem_info_c).wait()
+
+    devices = NW * NZ
 
     def arrange(k, _):
         src = source_of(k)
         tab[pl.ds(pl.multiple_of(src * NZ, NZ), NZ), :] = info_w[k, :, 0:clusters]
         for zz in range(NZ):
-            req[pl.ds(zz * NW + src, 1), :] = info_w[k, zz : zz + 1, clusters : clusters + 128]
+            row = (src % 2) * (devices // NC) + zz * (NX * NY) + src // 2
+            req[pl.ds(row, 1), :] = info_w[k, zz : zz + 1, clusters : clusters + 128]
         return 0
 
     lax.fori_loop(0, NW, arrange, 0)
@@ -254,9 +272,8 @@
         pos[2:3, cols] = jnp.where(gone, -1, true_parent)
         pos[3:4, cols] = true_parent
 
-    devices = NW * NZ
     place = iota((devices, 1), 0)
-    owner_of = (place % NW) * NZ + place // NW
+    owner_of = ((place % 16) * NC + place // 128) * NZ + (place // 16) % NZ
     ident = own[...] * clusters + slot[...]
     for k in range(2):
         asked = owner_of * clusters + req[:, 4 + k : 5 + k].astype(jnp.int32)
@@ -266,8 +283,14 @@
     true_parent = pos[3:4, :]
     by_z = jnp.where(iota((8, rows), 0) == true_parent // per_z, counts32, 0.0).astype(jnp.bfloat16)
     inside = (iota((per_z, rows), 0) == true_parent % per_z).astype(jnp.bfloat16)
-    red_z[0, :, 0 : 2 * devices] = nt_dot(counts8, onehot[...])
-    red_z[0, :, 2 * devices : 2 * devices + per_z] = nt_dot(by_z, inside)
+    asked_weights = nt_dot(counts8, onehot[...])
+    folded = jnp.zeros((8, 128), jnp.float32)
+    for i in range(2 * devices // 128):
+        folded = jnp.where(
+            iota((8, 128), 0) == i, asked_weights[:, i * 128 : (i + 1) * 128], folded
+        )
+    red_z[0, :, 0:128] = folded
+    red_z[0, :, 128 : 128 + per_z] = nt_dot(by_z, inside)
     spread_z(red_z.at[0], red_z, sem_red_z)
 
     def reduce_weights_z():
@@ -276,14 +299,21 @@
         for k in range(1, NZ):
             total = total + red_z[k]
         red_w[0] = total
-        spread_wide(red_w.at[0], red_w, sem_red_w)
+        spread_xy(red_w.at[0], red_w, sem_red_w)
 
     def reduce_weights_wide():
-        join_wide(red_w, sem_red_w)
+        join_xy(red_w, sem_red_w)
         total = red_w[0].astype(jnp.int32)
-        for k in range(1, NW):
+        for k in range(1, NX * NY):
             total = total + red_w[k].astype(jnp.int32)
-        totals[...] = total.astype(jnp.float32)
+        red_c[0] = total
+        swap = spread(red_c.at[0], red_c.at[1], sem_red_c, wide_peer((0, 0, 1)))
+        swap.start()
+        swap.wait()
+        total = (total + red_c[1]).astype(jnp.float32)
+        for i in range(2 * devices // 128):
+            totals[0:1, i * 128 : (i + 1) * 128] = total[i : i + 1, 0:128]
+        totals[:, 2 * devices : 2 * devices + per_z] = total[:, 128 : 128 + per_z]
 
     def pick_donors():
         first = (w * NZ + z) * rows
@@ -301,6 +331,12 @@
             return 0
 
         lax.fori_loop(0, width // tile, column, 0)
+        for k in range(2):
+            donors_copy(k).start()
+
+    def donors_copy(k):
+        at = pl.ds(pl.multiple_of(k * devices + (1 - c) * 128, 128), 128)
+        return spread(picked.at[at], donors_c.at[k], sem_donors_c, wide_peer((0, 0, 1)))
 
     def core_copy(s):
         b = lax.rem(s, 2)
@@ -377,7 +413,11 @@
         for h, blk in enumerate((block_f(s), block_b(s))):
             at = pl.ds(pl.multiple_of(c * mine, mine), mine)
             value = part[b, h, at, :] + core_recv[s, h]
-            chosen = picked[pl.ds(pl.multiple_of(h * devices + blk * NW, NW), NW), :]
+            at = pl.ds(pl.multiple_of(h * devices + c * 128 + blk * 16, 16), 16)
+            chosen = (
+                picked[at, :].astype(jnp.float32)
+                + donors_c[h, pl.ds(pl.multiple_of(blk * 16, 16), 16), :].astype(jnp.float32)
+            ).astype(jnp.bfloat16)
 
             @pl.when(s == 0)
             def _(h=h, value=value, chosen=chosen):
@@ -415,7 +455,7 @@
             rows_d[h] = ring_d[h, NZ - 1].astype(jnp.float32)
 
         def lay(k, _):
-            to = wide_index(offset(k))
+            to = wide_index(offset(k)) // NC
             for h in range(2):
                 for j in range(4):
                     send_d[k, 4 * h + j : 4 * h + j + 1, :] = rows_d[
@@ -423,27 +463,28 @@
                     ]
             return 0
 
-        lax.fori_loop(0, NW, lay, 0)
+        lax.fori_loop(0, NX * NY, lay, 0)
         recv_d[0] = send_d[0]
-        for d in WIDE_ORDER:
-            k = d[0] * 8 + d[1] * 2 + d[2]
-            spread(send_d.at[k], recv_d.at[k], sem_d, wide_peer(d)).start()
+        for dx, dy in XY_ORDER:
+            k = dx * NY + dy
+            spread(send_d.at[k], recv_d.at[k], sem_d, wide_peer((dx, dy, 0))).start()
 
     def join_three_and_donors():
-        at = pl.ds(1, NX * NY - 1)
-        spread(recv_xy.at[at], recv_xy.at[at], sem_xy, wide_peer((0, 1, 0))).wait()
+        join_xy(recv_xy, sem_xy)
         total = recv_xy[0]
         for k in range(1, NX * NY):
             total = total + recv_xy[k]
         recv_three[0] = total
-        join_wide(recv_d, sem_d)
+        join_xy(recv_d, sem_d)
         total = recv_d[0]
-        for k in range(1, NW):
+        for k in range(1, NX * NY):
             total = total + recv_d[k]
         final_d[...] = total
 
     def finish_three():
-        join_wide(recv_three, sem_three)
+        join_xy(recv_three, sem_three)
+        to_core(recv_three, sem_three_c).start()
+        to_core(recv_three, sem_three_c).wait()
 
         def lay(k, _):
             src = source_of(k)
@@ -479,10 +520,10 @@
             acc_four[...] += recv_four[(z + NZ - zz) % NZ]
         mass = jnp.maximum(acc_four[:, width : width + 1], 1.0)
         recv_out[0] = acc_four[:, 0:width] / mass
-        spread_wide(recv_out.at[0], recv_out, sem_out)
+        spread_xy(recv_out.at[0], recv_out, sem_out)
 
     def finish_four():
-        join_wide(recv_out, sem_out)
+        to_core(recv_out, sem_out_c).wait()
 
         def lay(k, _):
             out4[pl.ds(pl.multiple_of(source_of(k) * 8, 8), 8), :] = recv_out[k]
@@ -490,47 +531,60 @@
 
         lax.fori_loop(0, NW, lay, 0)
 
-    def ring_copy(ring, t, sems, k):
+    def q_copy(h, t):
         return pltpu.make_async_remote_copy(
-            src_ref=ring.at[t], dst_ref=ring.at[t + 1],
-            send_sem=sems[0].at[t], recv_sem=sems[1].at[t + 1],
-            device_id=z_peer(k), device_id_type=MESH,
-        )
-
-    rings = (
-        (ring_f, (f_send, f_recv), 1, block_f),
-        (ring_b, (b_send, b_recv), NZ - 1, block_b),
-    )
+            src_ref=ring_q.at[h, t], dst_ref=ring_q.at[h, t + 1],
+            send_sem=q_send.at[h, t], recv_sem=q_recv.at[h, t + 1],
+            device_id=z_peer((1, NZ - 1)[h]), device_id_type=MESH,
+        )
+
+    def s_copy(h, t):
+        return pltpu.make_async_remote_copy(
+            src_ref=ring_s.at[h, t], dst_ref=ring_s.at[h, t + 1],
+            send_sem=sc_send.at[h, t], recv_sem=sc_recv.at[h, t + 1],
+            device_id=z_peer((1, NZ - 1)[h]), device_id_type=MESH,
+        )
+
+    groups = half // 128
+
+    def take_in(h, t):
+        q_copy(h, t - 1).wait_recv()
+        s_copy(h, t - 1).wait_recv()
+        turn[0:8, :] = ring_s[h, t]
+        scale = jnp.transpose(turn[...]) * (1.0 / TOP)
+        for j in range(groups):
+            at = slice(j * 128, (j + 1) * 128)
+            value = ring_q[h, t, :, at].astype(jnp.int32).astype(jnp.float32)
+            acc[h, :, at] += value * scale[:, j : j + 1]
+
+    def pass_on(h, t):
+        scale = jnp.zeros((clusters, 128), jnp.float32)
+        for j in range(groups):
+            at = slice(j * 128, (j + 1) * 128)
+            value = acc[h, :, at]
+            top = jnp.maximum(jnp.max(jnp.abs(value), axis=1, keepdims=True), 1e-37)
+            scale = jnp.where(iota((clusters, 128), 1) == j, top, scale)
+            ring_q[h, t, :, at] = (
+                jnp.round(value * (1.0 / top) * TOP).astype(jnp.int32).astype(jnp.int16)
+            )
+        ring_s[h, t] = jnp.transpose(scale)[0:8, :]
+        q_copy(h, t).start()
+        s_copy(h, t).start()
 
     def reduce_stage(t):
         all_wide(sbuf.at[0], rbuf.at[t], s_sem.at[0], r_sem.at[t]).wait_recv()
-        for h, (ring, sems, k, block) in enumerate(rings):
-            hit, counts = matched(block(t))
+        for h, blk in enumerate((block_f(t), block_b(t))):
+            hit, counts = matched(blk)
             assign = jnp.where(hit, counts, 0.0).astype(jnp.bfloat16)
-
-            @pl.when(t > 0)
-            def _(ring=ring, sems=sems, k=k):
-                ring_copy(ring, t - 1, sems, k).wait_recv()
-
             for n in range(half // tile):
-                at = slice(n * tile, (n + 1) * tile)
-                value = jnp.dot(
+                acc[h, :, n * tile : (n + 1) * tile] = jnp.dot(
                     assign,
                     rbuf[t, :, h * half + n * tile : h * half + (n + 1) * tile],
                     preferred_element_type=jnp.float32,
                 )
-
-                @pl.when(t == 0)
-                def _(ring=ring, at=at, value=value):
-                    ring[t, :, at] = value
-
-                @pl.when(t > 0)
-                def _(ring=ring, at=at, value=value):
-                    ring[t, :, at] += value
-
-            @pl.when(t < NZ - 1)
-            def _(ring=ring, sems=sems, k=k):
-                ring_copy(ring, t, sems, k).start()
+        for h in range(2):
+            pl.when(t > 0)(lambda h=h: take_in(h, t))
+            pl.when(t < NZ - 1)(lambda h=h: pass_on(h, t))
 
     def at_stage(t, which, work):
         pl.when(t == which)(work)
@@ -544,11 +598,11 @@
 
         @pl.when((t >= 1) & (t <= 4))
         def _():
-            step_three(2 * t - 2)
-
-        at_stage(t, 5, send_three_and_donors)
-        at_stage(t, 6, lambda: spread_wide(recv_three.at[0], recv_three, sem_three))
-        at_stage(t, 7, send_four)
+            step_three(2 * t - 1)
+
+        at_stage(t, 4, send_three_and_donors)
+        at_stage(t, 5, lambda: spread_xy(recv_three.at[0], recv_three, sem_three))
+        at_stage(t, 6, send_four)
 
         @pl.when(t < NZ - 1)
         def _():
@@ -561,13 +615,20 @@
             reduce_weights_wide()
             pick_donors()
             local_three(0)
-
-        @pl.when((t >= 1) & (t <= 4))
-        def _():
-            step_three(2 * t - 1)
-
-        at_stage(t, 5, join_three_and_donors)
-        at_stage(t, 6, finish_three)
+            spread(donors_c, donors_c, sem_donors_c, wide_peer((0, 0, 1))).wait()
+
+        @pl.when(t <= 3)
+        def _():
+            step_three(2 * t)
+
+        at_stage(t, 4, join_three_and_donors)
+        at_stage(t, 5, finish_three)
+
+        @pl.when(t == 6)
+        def _():
+            join_xy(recv_out, sem_out)
+            to_core(recv_out, sem_out_c).start()
+
         return 0
 
     lax.fori_loop(0, NZ, stage, 0)
@@ -582,9 +643,8 @@
     mass = jnp.maximum(mass, 1.0)
     seeded = [iota((clusters, 1), 0) == reseed[0:1, k : k + 1] for k in range(2)]
     for j in range(4):
-        ring = rings[j // 2][0]
         at = (j % 2) * quarter
-        value = ring[NZ - 1, :, at : at + quarter] / mass
+        value = acc[j // 2, :, at : at + quarter] / mass
         for k in range(2):
             value = jnp.where(seeded[k], final_d[4 * k + j : 4 * k + j + 1, :], value)
         out2[:, j * quarter : (j + 1) * quarter] = value
@@ -596,8 +656,9 @@
         core_copy(b).wait_send()
 
     def drain(t, _):
-        for h, (ring, sems, k, block) in enumerate(rings):
-            ring_copy(ring, t, sems, k).wait_send()
+        for h in range(2):
+            q_copy(h, t).wait_send()
+            s_copy(h, t).wait_send()
             ring3_copy(h, t).wait_send()
             ring_d_copy(h, t).wait_send()
         return 0
@@ -631,9 +692,10 @@
             jax.ShapeDtypeStruct((per_z, width), f32),
             jax.ShapeDtypeStruct((L4, width), f32),
         ),
-        in_specs=[vmem] * 8,
+        in_specs=[pl.BlockSpec(memory_space=pl.ANY)] + [vmem] * 7,
         out_specs=(vmem,) * 3,
         scratch_shapes=[
+            pltpu.VMEM((rows, width), bf16),
             pltpu.VMEM((SEND_BUFFERS, places, width), bf16),
             pltpu.VMEM((NZ, places, width), bf16),
             pltpu.VMEM((places, rows), bf16),
@@ -641,26 +703,30 @@
             pltpu.VMEM((places, 128), bf16),
             pltpu.VMEM((places, 128), bf16),
             pltpu.VMEM((16, places), f32),
-            pltpu.VMEM((NZ, clusters, half), f32),
-            pltpu.VMEM((NZ, clusters, half), f32),
+            pltpu.VMEM((2, NZ, clusters, half), jnp.int16),
+            pltpu.VMEM((2, NZ, 8, clusters), f32),
+            pltpu.VMEM((2, clusters, half), f32),
+            pltpu.VMEM((128, clusters), f32),
             pltpu.VMEM((NZ, 8, clusters), f32),
             pltpu.VMEM((NZ, 8, clusters), f32),
             pltpu.VMEM((NZ, NZ, clusters + 128), f32),
             pltpu.VMEM((NW, NZ, clusters + 128), f32),
             pltpu.VMEM((devices, clusters), f32),
             pltpu.VMEM((devices, 128), f32),
-            pltpu.VMEM((NZ, 8, 2 * devices + per_z), f32),
-            pltpu.VMEM((NW, 8, 2 * devices + per_z), f32),
+            pltpu.VMEM((NZ, 8, 128 + per_z), f32),
+            pltpu.VMEM((NX * NY, 8, 128 + per_z), f32),
+            pltpu.VMEM((2, 8, 128 + per_z), jnp.int32),
             pltpu.VMEM((8, 2 * devices + per_z), f32),
             pltpu.VMEM((2 * devices, width), bf16),
+            pltpu.VMEM((2, devices // NC, width), bf16),
             pltpu.VMEM((2, 2, per_z, half), f32),
             pltpu.VMEM((2, 2, per_z // NC, half), f32),
             pltpu.VMEM((NZ, 2, per_z // NC, half), f32),
             pltpu.VMEM((2, NZ, per_z // NC, half), f32),
-            pltpu.VMEM((2, NZ, NW, width), bf16),
-            pltpu.VMEM((2, NW, width), f32),
-            pltpu.VMEM((NW, 8, width // 4), f32),
-            pltpu.VMEM((NW, 8, width // 4), f32),
+            pltpu.VMEM((2, NZ, NX * NY, width), bf16),
+            pltpu.VMEM((2, NX * NY, width), f32),
+            pltpu.VMEM((NX * NY, 8, width // 4), f32),
+            pltpu.VMEM((NX * NY, 8, width // 4), f32),
             pltpu.VMEM((8, width // 4), f32),
             pltpu.VMEM((NX * NY, 8, half), f32),
             pltpu.VMEM((NW, 8, half), f32),
@@ -668,13 +734,14 @@
             pltpu.VMEM((NZ, 8, width + 128), f32),
             pltpu.VMEM((NW, 8, width), f32),
             pltpu.VMEM((8, width + 128), f32),
+            dma((1,)),
             dma((SEND_BUFFERS,)),
             dma((NZ,)),
-            dma((NZ,)),
-            dma((NZ,)),
-            dma((NZ,)),
-            dma((NZ,)),
-            dma((11, 2)),
+            dma((2, NZ)),
+            dma((2, NZ)),
+            dma((2, NZ)),
+            dma((2, NZ)),
+            dma((16, 2)),
             dma((2,)),
             dma((NZ,)),
             dma((2, NZ)),

time: 271 us -> 209 us (0.77); the launches traced: 267 us -> 209 us
  Pallas kernels: 261 us -> 203 us
    pallas_call x1, Pallas kernels: 261 us -> 203 us  [per_device(): pl.pallas_call(centroid_kernel, out_shape=(jax.ShapeDtypeStruct((clusters...]
where the time goes in v3:
time: 209 us
  Pallas kernels  203 us (97%)
  local copies, waits for them, and re-layouts  5.57 us (3%)
    pallas_call x1, Pallas kernels, per_device(): pl.pallas_call(centroid_kernel, out_shape=(jax.ShapeDtypeStruct((clusters...  203 us
    unnamed x7, local copies, waits for them, and re-layouts  5.57 us

profile of v3, /device:TPU:1, one launch (start us, length us, event | category | flops | bytes accessed | tf_op | source)
XLA Modules:
  0.0 209.0 jit_solution(18380802583572630574)
XLA Ops:
  0.6 202.8 %shard_map.103 = (f32[256,1536]{1,0:T(8,128)}, f32[128,1536]{1,0:T(8,128)}, f32[256,1536]{1,0:T(8,128)}) custom-call(bf16[2048,1536]{1,0:T(8,128)(2,1)} %emb_hbm.1, s32[1,2048]{1,0:T(1,128)} %bitcast.5, s32[1,2048]{1,0:T(1,128)} %bitcast.6, s32[1,2048]{1,0:T(1,128)} %bitcast.7, s32[1,256]{1,0:T(1,128)} %bitcast.8, s32[1,128]{1,0:T(1,128)} %bitcast.9, ...), custom_call_target="tpu_custom_call" | custom-call | tf_op jit(solution)/shard_map/pallas_call | solution.py:688
  203.4 0.0 copy-start.1
  203.4 2.7 %copy.14 = f32[256,1536]{1,0:T(8,128)} copy(f32[256,1536]{1,0:T(8,128)} %get-tuple-element.6) | data formatting | bytes 3145728
  206.1 0.0 copy-done.1
  206.1 0.0 copy-start
  206.2 0.9 copy.15
  207.0 0.8 copy-done
  207.8 1.1 copy.16
Async XLA Ops:
  203.4 2.7 %copy-start.1 = (f32[128,1536]{1,0:T(8,128)S(1)}, f32[128,1536]{1,0:T(8,128)}, u32[]{:S(2)}) copy-start(f32[128,1536]{1,0:T(8,128)} %get-tuple-element.7) | copy-start | bytes 2359300
  206.1 1.7 copy-start

commit v4 on v3

--- a/solution.py
+++ b/solution.py
@@ -37,11 +37,11 @@
 def centroid_kernel(
     emb_hbm, own, slot, cnt, par2, par3, reseed, donor,
     out2, out3, out4,
-    emb, sbuf, rbuf, onehot, pos, lab_send, lab_recv, lab_t, ring_q, ring_s, acc, turn, w_send, w_recv,
+    emb, sbuf, rbuf, onehot, pos, lab_send, lab_recv, lab_t, ring_q, ring_s, acc, turn, mass_two, w_send, w_recv,
     info_z, info_w, tab, req, red_z, red_w, red_c, totals, picked, donors_c,
-    part, core_send, core_recv, ring3, ring_d, rows_d, send_d, recv_d, final_d,
+    part, core_send, core_recv, three_q, three_s, acc3, turn3, ring_d, rows_d, send_d, recv_d, final_d,
     recv_xy, recv_three, three, recv_four, recv_out, acc_four,
-    load_sem, s_sem, r_sem, q_send, q_recv, sc_send, sc_recv, once, core_s, core_r, s3_sem, r3_sem,
+    load_sem, s_sem, r_sem, q_send, q_recv, sc_send, sc_recv, once, core_s, core_r, s3_sem, r3_sem, sc3_send, sc3_recv,
     sd_sem, rd_sem,
 ):
     load = pltpu.make_async_copy(emb_hbm, emb, load_sem.at[0])
@@ -122,6 +122,9 @@
         extra = jnp.where(lane == i, v.astype(jnp.float32), extra)
     info_z[0, :, 0:clusters] = jnp.where(iota((NZ, clusters), 0) == z, table, 0.0)
     info_z[0, :, clusters : clusters + 128] = jnp.where(iota((NZ, 128), 0) == z, extra, 0.0)
+
+    pl.semaphore_wait(barrier, NW - 1 + NZ - 1)
+    spread_z(info_z.at[0], info_z, sem_info_z)
 
     owner = own[...]
     target = owner // NZ
@@ -142,8 +145,6 @@
         pos[0:1, cols] = rel[:, cols] * CAP + rank.astype(jnp.int32)
     pos[1:2, :] = owner % NZ
 
-    pl.semaphore_wait(barrier, NW - 1 + NZ - 1)
-    spread_z(info_z.at[0], info_z, sem_info_z)
 
     places = NW * CAP
     tile = 256
@@ -152,15 +153,6 @@
         for i in range(places // tile):
             ids = iota((tile, rows), 0) + i * tile
             onehot[i * tile : (i + 1) * tile, :] = (ids == where_row).astype(jnp.bfloat16)
-
-    fill_onehot(pos[0:1, :])
-    deep = iota((128, rows), 0)
-    z_of = pos[1:2, :]
-    labels = jnp.where(
-        deep == 2 * z_of, slot[...], jnp.where(deep == 2 * z_of + 1, cnt[...], 0)
-    ).astype(jnp.float32).astype(jnp.bfloat16)
-    lab_send[...] = nt_dot(onehot[...], labels).astype(jnp.bfloat16)
-    lab_recv[0:CAP, :] = lab_send[0:CAP, :]
 
     def send_wide(src, dst, sem_s, sem_r):
         for d in WIDE_ORDER:
@@ -177,7 +169,6 @@
             device_id=wide_peer((0, 0, 1)), device_id_type=MESH,
         )
 
-    send_wide(lab_send, lab_recv, sem_lab.at[0], sem_lab.at[1])
 
     def block_f(t):
         return (z + 2 * NZ - 1 - t) % NZ
@@ -185,6 +176,20 @@
     def block_b(t):
         return (z + 1 + t) % NZ
 
+    def pack_half(t, h):
+        b = lax.rem(t, SEND_BUFFERS)
+        blk = (block_f, block_b)[h](t)
+        fill_onehot(jnp.where(pos[1:2, :] == blk, pos[0:1, :], -1))
+
+        def column(n, _):
+            at = pl.ds(pl.multiple_of(h * half + n * tile, tile), tile)
+            sbuf[b, :, at] = jnp.dot(
+                onehot[...], emb[:, at], preferred_element_type=jnp.float32
+            ).astype(jnp.bfloat16)
+            return 0
+
+        lax.fori_loop(0, half // tile, column, 0)
+
     def pack(t):
         b = lax.rem(t, SEND_BUFFERS)
 
@@ -192,39 +197,35 @@
         def _():
             all_wide(sbuf.at[b], rbuf.at[t], s_sem.at[b], r_sem.at[t]).wait_send()
 
-        for h, blk in enumerate((block_f(t), block_b(t))):
-            fill_onehot(jnp.where(pos[1:2, :] == blk, pos[0:1, :], -1))
-
-            def column(n, _, h=h):
-                at = pl.ds(pl.multiple_of(h * half + n * tile, tile), tile)
-                sbuf[b, :, at] = jnp.dot(
-                    onehot[...], emb[:, at], preferred_element_type=jnp.float32
-                ).astype(jnp.bfloat16)
-                return 0
-
-            lax.fori_loop(0, half // tile, column, 0)
+        for h in range(2):
+            pack_half(t, h)
         rbuf[t, 0:CAP, :] = sbuf[b, 0:CAP, :]
 
     def send(t):
         b = lax.rem(t, SEND_BUFFERS)
         send_wide(sbuf.at[b], rbuf.at[t], s_sem.at[b], r_sem.at[t])
 
-    load.wait()
-    pack(0)
     join_z(info_z, sem_info_z)
     whole = info_z[0]
     for k in range(1, NZ):
         whole = whole + info_z[k]
     info_w[0] = whole
     spread_xy(info_w.at[0], info_w, sem_info_w)
-    send(0)
-
-    turn[...] = jnp.zeros(turn.shape, jnp.float32)
+    load.wait()
+    pack_half(0, 0)
     join_xy(info_w, sem_info_w)
     to_core(info_w, sem_info_c).start()
-    all_wide(lab_send, lab_recv, sem_lab.at[0], sem_lab.at[1]).wait()
-    eye = (iota((16, 128), 0) == iota((16, 128), 1)).astype(jnp.bfloat16)
-    lab_t[...] = nt_dot(eye, lab_recv[...])
+    pack_half(0, 1)
+    rbuf[0, 0:CAP, :] = sbuf[0, 0:CAP, :]
+    send(0)
+
+    turn[...] = jnp.zeros(turn.shape, jnp.float32)
+    turn3[...] = jnp.zeros(turn3.shape, jnp.float32)
+
+    def turn_labels():
+        all_wide(lab_send, lab_recv, sem_lab.at[0], sem_lab.at[1]).wait()
+        eye = (iota((16, 128), 0) == iota((16, 128), 1)).astype(jnp.bfloat16)
+        lab_t[...] = nt_dot(eye, lab_recv[...])
 
     def matched(blk):
         ids = iota((clusters, places), 0).astype(jnp.float32)
@@ -236,9 +237,20 @@
         w_send[k] = nt_dot(counts, hit.astype(jnp.float32).astype(jnp.bfloat16))
         return 0
 
-    lax.fori_loop(0, NZ, weigh, 0)
-    for k in range(1, NZ):
-        spread(w_send.at[k], w_recv.at[k], sem_w, z_peer(k)).start()
+    def send_masses():
+        lax.fori_loop(0, NZ, weigh, 0)
+        for k in range(1, NZ):
+            spread(w_send.at[k], w_recv.at[k], sem_w, z_peer(k)).start()
+
+    def join_masses():
+        others = pl.ds(1, NZ - 1)
+        spread(w_send.at[others], w_recv.at[others], sem_w, z_peer(1)).wait()
+        total = w_send[0]
+        for k in range(1, NZ):
+            total = total + w_recv[k]
+        diagonal = iota((clusters, clusters), 0) == iota((clusters, clusters), 1)
+        mass = jnp.sum(jnp.where(diagonal, total[0:1, :], 0.0), axis=1, keepdims=True)
+        mass_two[...] = jnp.broadcast_to(jnp.maximum(mass, 1.0), mass_two.shape)
 
     to_core(info_w, sem_info_c).wait()
 
@@ -292,6 +304,16 @@
     red_z[0, :, 0:128] = folded
     red_z[0, :, 128 : 128 + per_z] = nt_dot(by_z, inside)
     spread_z(red_z.at[0], red_z, sem_red_z)
+
+    fill_onehot(pos[0:1, :])
+    deep = iota((128, rows), 0)
+    z_of = pos[1:2, :]
+    labels = jnp.where(
+        deep == 2 * z_of, slot[...], jnp.where(deep == 2 * z_of + 1, cnt[...], 0)
+    ).astype(jnp.float32).astype(jnp.bfloat16)
+    lab_send[...] = nt_dot(onehot[...], labels).astype(jnp.bfloat16)
+    lab_recv[0:CAP, :] = lab_send[0:CAP, :]
+    send_wide(lab_send, lab_recv, sem_lab.at[0], sem_lab.at[1])
 
     def reduce_weights_z():
         join_z(red_z, sem_red_z)
@@ -389,12 +411,61 @@
             core_send[b, h] = part[b, h, pl.ds(pl.multiple_of((1 - c) * mine, mine), mine), :]
         core_copy(s).start()
 
-    def ring3_copy(h, s):
-        return pltpu.make_async_remote_copy(
-            src_ref=ring3.at[h, s], dst_ref=ring3.at[h, s + 1],
-            send_sem=s3_sem.at[h, s], recv_sem=r3_sem.at[h, s + 1],
-            device_id=z_peer((1, NZ - 1)[h]), device_id_type=MESH,
-        )
+    groups = half // 128
+
+    def fixed_ring(q, sc, total, turned, q_sems, sc_sems):
+        rows_in, lanes = total.shape[1], turned.shape[1]
+
+        def copies(h, t):
+            to = z_peer((1, NZ - 1)[h])
+            return [
+                pltpu.make_async_remote_copy(
+                    src_ref=ref.at[h, t], dst_ref=ref.at[h, t + 1],
+                    send_sem=sems[0].at[h, t], recv_sem=sems[1].at[h, t + 1],
+                    device_id=to, device_id_type=MESH,
+                )
+                for ref, sems in ((q, q_sems), (sc, sc_sems))
+            ]
+
+        def take_in(h, t):
+            for copy in copies(h, t - 1):
+                copy.wait_recv()
+            turned[0:8, :] = sc[h, t]
+            scale = jnp.transpose(turned[...])[0:rows_in, :] * (1.0 / TOP)
+            for j in range(groups):
+                at = slice(j * 128, (j + 1) * 128)
+                value = q[h, t, :, at].astype(jnp.int32).astype(jnp.float32)
+                total[h, :, at] += value * scale[:, j : j + 1]
+
+        def pass_on(h, t):
+            scale = jnp.zeros((rows_in, 128), jnp.float32)
+            for j in range(groups):
+                at = slice(j * 128, (j + 1) * 128)
+                value = total[h, :, at]
+                top = jnp.maximum(jnp.max(jnp.abs(value), axis=1, keepdims=True), 1e-37)
+                scale = jnp.where(iota((rows_in, 128), 1) == j, top, scale)
+                q[h, t, :, at] = (
+                    jnp.round(value * (1.0 / top) * TOP).astype(jnp.int32).astype(jnp.int16)
+                )
+            if rows_in < lanes:
+                filler = jnp.zeros((lanes - rows_in, 128), jnp.float32)
+                scale = jnp.concatenate([scale, filler], axis=0)
+            sc[h, t] = jnp.transpose(scale)[0:8, :]
+            for copy in copies(h, t):
+                copy.start()
+
+        def drain(h, t):
+            for copy in copies(h, t):
+                copy.wait_send()
+
+        return take_in, pass_on, drain
+
+    take_in, pass_on, drain_two = fixed_ring(
+        ring_q, ring_s, acc, turn, (q_send, q_recv), (sc_send, sc_recv)
+    )
+    take_three, pass_three, drain_three = fixed_ring(
+        three_q, three_s, acc3, turn3, (s3_sem, r3_sem), (sc3_send, sc3_recv)
+    )
 
     def ring_d_copy(h, s):
         return pltpu.make_async_remote_copy(
@@ -412,7 +483,7 @@
         core_copy(s).wait_recv()
         for h, blk in enumerate((block_f(s), block_b(s))):
             at = pl.ds(pl.multiple_of(c * mine, mine), mine)
-            value = part[b, h, at, :] + core_recv[s, h]
+            acc3[h] = part[b, h, at, :] + core_recv[s, h]
             at = pl.ds(pl.multiple_of(h * devices + c * 128 + blk * 16, 16), 16)
             chosen = (
                 picked[at, :].astype(jnp.float32)
@@ -420,14 +491,12 @@
             ).astype(jnp.bfloat16)
 
             @pl.when(s == 0)
-            def _(h=h, value=value, chosen=chosen):
-                ring3[h, s] = value
+            def _(h=h, chosen=chosen):
                 ring_d[h, s] = chosen
 
             @pl.when(s > 0)
-            def _(h=h, value=value, chosen=chosen):
-                ring3_copy(h, s - 1).wait_recv()
-                ring3[h, s] += value
+            def _(h=h, chosen=chosen):
+                take_three(h, s)
                 ring_d_copy(h, s - 1).wait_recv()
                 ring_d[h, s] = (
                     ring_d[h, s].astype(jnp.float32) + chosen.astype(jnp.float32)
@@ -435,14 +504,14 @@
 
             @pl.when(s < NZ - 1)
             def _(h=h):
-                ring3_copy(h, s).start()
+                pass_three(h, s)
                 ring_d_copy(h, s).start()
 
     quarter = width // 4
 
     def piece(xx, yy):
         i = xx * NY + yy
-        return ring3.at[i // 8, NZ - 1, pl.ds(pl.multiple_of((i % 8) * 8, 8), 8)]
+        return acc3.at[i // 8, pl.ds(pl.multiple_of((i % 8) * 8, 8), 8)]
 
     def send_three_and_donors():
         recv_xy[0] = piece(x, y)[...]
@@ -531,46 +600,6 @@
 
         lax.fori_loop(0, NW, lay, 0)
 
-    def q_copy(h, t):
-        return pltpu.make_async_remote_copy(
-            src_ref=ring_q.at[h, t], dst_ref=ring_q.at[h, t + 1],
-            send_sem=q_send.at[h, t], recv_sem=q_recv.at[h, t + 1],
-            device_id=z_peer((1, NZ - 1)[h]), device_id_type=MESH,
-        )
-
-    def s_copy(h, t):
-        return pltpu.make_async_remote_copy(
-            src_ref=ring_s.at[h, t], dst_ref=ring_s.at[h, t + 1],
-            send_sem=sc_send.at[h, t], recv_sem=sc_recv.at[h, t + 1],
-            device_id=z_peer((1, NZ - 1)[h]), device_id_type=MESH,
-        )
-
-    groups = half // 128
-
-    def take_in(h, t):
-        q_copy(h, t - 1).wait_recv()
-        s_copy(h, t - 1).wait_recv()
-        turn[0:8, :] = ring_s[h, t]
-        scale = jnp.transpose(turn[...]) * (1.0 / TOP)
-        for j in range(groups):
-            at = slice(j * 128, (j + 1) * 128)
-            value = ring_q[h, t, :, at].astype(jnp.int32).astype(jnp.float32)
-            acc[h, :, at] += value * scale[:, j : j + 1]
-
-    def pass_on(h, t):
-        scale = jnp.zeros((clusters, 128), jnp.float32)
-        for j in range(groups):
-            at = slice(j * 128, (j + 1) * 128)
-            value = acc[h, :, at]
-            top = jnp.maximum(jnp.max(jnp.abs(value), axis=1, keepdims=True), 1e-37)
-            scale = jnp.where(iota((clusters, 128), 1) == j, top, scale)
-            ring_q[h, t, :, at] = (
-                jnp.round(value * (1.0 / top) * TOP).astype(jnp.int32).astype(jnp.int16)
-            )
-        ring_s[h, t] = jnp.transpose(scale)[0:8, :]
-        q_copy(h, t).start()
-        s_copy(h, t).start()
-
     def reduce_stage(t):
         all_wide(sbuf.at[0], rbuf.at[t], s_sem.at[0], r_sem.at[t]).wait_recv()
         for h, blk in enumerate((block_f(t), block_b(t))):
@@ -596,24 +625,35 @@
 
         at_stage(t, 0, reduce_weights_z)
 
-        @pl.when((t >= 1) & (t <= 4))
+        @pl.when(t == 4)
         def _():
             step_three(2 * t - 1)
-
-        at_stage(t, 4, send_three_and_donors)
+            send_three_and_donors()
+
         at_stage(t, 5, lambda: spread_xy(recv_three.at[0], recv_three, sem_three))
+
+        @pl.when(t < NZ - 1)
+        def _():
+            send(t + 1)
+
+        @pl.when(t == 0)
+        def _():
+            pick_donors()
+            turn_labels()
+
+        at_stage(t, 1, send_masses)
+
+        @pl.when((t >= 1) & (t <= 3))
+        def _():
+            step_three(2 * t - 1)
+
         at_stage(t, 6, send_four)
-
-        @pl.when(t < NZ - 1)
-        def _():
-            send(t + 1)
-
+        at_stage(t, 7, join_masses)
         reduce_stage(t)
 
         @pl.when(t == 0)
         def _():
             reduce_weights_wide()
-            pick_donors()
             local_three(0)
             spread(donors_c, donors_c, sem_donors_c, wide_peer((0, 0, 1))).wait()
 
@@ -623,24 +663,11 @@
 
         at_stage(t, 4, join_three_and_donors)
         at_stage(t, 5, finish_three)
-
-        @pl.when(t == 6)
-        def _():
-            join_xy(recv_out, sem_out)
-            to_core(recv_out, sem_out_c).start()
-
         return 0
 
     lax.fori_loop(0, NZ, stage, 0)
 
-    others = pl.ds(1, NZ - 1)
-    spread(w_send.at[others], w_recv.at[others], sem_w, z_peer(1)).wait()
-    total = w_send[0]
-    for k in range(1, NZ):
-        total = total + w_recv[k]
-    diagonal = iota((clusters, clusters), 0) == iota((clusters, clusters), 1)
-    mass = jnp.sum(jnp.where(diagonal, total[0:1, :], 0.0), axis=1, keepdims=True)
-    mass = jnp.maximum(mass, 1.0)
+    mass = mass_two[:, 0:1]
     seeded = [iota((clusters, 1), 0) == reseed[0:1, k : k + 1] for k in range(2)]
     for j in range(4):
         at = (j % 2) * quarter
@@ -649,6 +676,8 @@
             value = jnp.where(seeded[k], final_d[4 * k + j : 4 * k + j + 1, :], value)
         out2[:, j * quarter : (j + 1) * quarter] = value
 
+    join_xy(recv_out, sem_out)
+    to_core(recv_out, sem_out_c).start()
     finish_four()
     for b in range(SEND_BUFFERS):
         all_wide(sbuf.at[b], rbuf.at[0], s_sem.at[b], r_sem.at[0]).wait_send()
@@ -657,9 +686,8 @@
 
     def drain(t, _):
         for h in range(2):
-            q_copy(h, t).wait_send()
-            s_copy(h, t).wait_send()
-            ring3_copy(h, t).wait_send()
+            drain_two(h, t)
+            drain_three(h, t)
             ring_d_copy(h, t).wait_send()
         return 0
 
@@ -707,6 +735,7 @@
             pltpu.VMEM((2, NZ, 8, clusters), f32),
             pltpu.VMEM((2, clusters, half), f32),
             pltpu.VMEM((128, clusters), f32),
+            pltpu.VMEM((clusters, 128), f32),
             pltpu.VMEM((NZ, 8, clusters), f32),
             pltpu.VMEM((NZ, 8, clusters), f32),
             pltpu.VMEM((NZ, NZ, clusters + 128), f32),
@@ -722,7 +751,10 @@
             pltpu.VMEM((2, 2, per_z, half), f32),
             pltpu.VMEM((2, 2, per_z // NC, half), f32),
             pltpu.VMEM((NZ, 2, per_z // NC, half), f32),
-            pltpu.VMEM((2, NZ, per_z // NC, half), f32),
+            pltpu.VMEM((2, NZ, per_z // NC, half), jnp.int16),
+            pltpu.VMEM((2, NZ, 8, 128), f32),
+            pltpu.VMEM((2, per_z // NC, half), f32),
+            pltpu.VMEM((128, 128), f32),
             pltpu.VMEM((2, NZ, NX * NY, width), bf16),
             pltpu.VMEM((2, NX * NY, width), f32),
             pltpu.VMEM((NX * NY, 8, width // 4), f32),
@@ -744,6 +776,8 @@
             dma((16, 2)),
             dma((2,)),
             dma((NZ,)),
+            dma((2, NZ)),
+            dma((2, NZ)),
             dma((2, NZ)),
             dma((2, NZ)),
             dma((2, NZ)),

time: 209 us -> 203 us (0.971)
  Pallas kernels: 203 us -> 196 us
    pallas_call x1, Pallas kernels: 203 us -> 196 us  [per_device(): pl.pallas_call(centroid_kernel, out_shape=(jax.ShapeDtypeStruct((clusters...]
where the time goes in v4:
time: 203 us; the launch traced here: 202 us
  Pallas kernels  196 us (97%)
  local copies, waits for them, and re-layouts  5.57 us (3%)
    pallas_call x1, Pallas kernels, per_device(): pl.pallas_call(centroid_kernel, out_shape=(jax.ShapeDtypeStruct((clusters...  196 us
    unnamed x7, local copies, waits for them, and re-layouts  5.57 us

profile of v4, /device:TPU:1, one launch (start us, length us, event | category | flops | bytes accessed | tf_op | source)
XLA Modules:
  0.0 202.4 jit_solution(3038088450378093957)
XLA Ops:
  0.6 196.2 %shard_map.103 = (f32[256,1536]{1,0:T(8,128)}, f32[128,1536]{1,0:T(8,128)}, f32[256,1536]{1,0:T(8,128)}) custom-call(bf16[2048,1536]{1,0:T(8,128)(2,1)} %emb_hbm.1, s32[1,2048]{1,0:T(1,128)} %bitcast.5, s32[1,2048]{1,0:T(1,128)} %bitcast.6, s32[1,2048]{1,0:T(1,128)} %bitcast.7, s32[1,256]{1,0:T(1,128)} %bitcast.8, s32[1,128]{1,0:T(1,128)} %bitcast.9, ...), custom_call_target="tpu_custom_call" | custom-call | tf_op jit(solution)/shard_map/pallas_call | solution.py:716
  196.8 0.0 copy-start.1
  196.8 2.7 %copy.14 = f32[256,1536]{1,0:T(8,128)} copy(f32[256,1536]{1,0:T(8,128)} %get-tuple-element.6) | data formatting | bytes 3145728
  199.6 0.0 copy-done.1
  199.6 0.0 copy-start
  199.6 0.9 copy.15
  200.4 0.8 copy-done
  201.2 1.1 copy.16
Async XLA Ops:
  196.8 2.7 %copy-start.1 = (f32[128,1536]{1,0:T(8,128)S(1)}, f32[128,1536]{1,0:T(8,128)}, u32[]{:S(2)}) copy-start(f32[128,1536]{1,0:T(8,128)} %get-tuple-element.7) | copy-start | bytes 2359300
  199.6 1.7 copy-start

commit v5 on v4

--- a/solution.py
+++ b/solution.py
@@ -155,11 +155,13 @@
             onehot[i * tile : (i + 1) * tile, :] = (ids == where_row).astype(jnp.bfloat16)
 
     def send_wide(src, dst, sem_s, sem_r):
+        sign = 1 - 2 * c
         for d in WIDE_ORDER:
-            at = pl.ds(rel_of(d) * CAP, CAP)
+            to = ((d[0] * sign + NX) % NX, (d[1] * sign + NY) % NY, d[2])
+            at = pl.ds(pl.multiple_of(rel_of(to) * CAP, CAP), CAP)
             pltpu.make_async_remote_copy(
                 src_ref=src.at[at], dst_ref=dst.at[at], send_sem=sem_s, recv_sem=sem_r,
-                device_id=wide_peer(d), device_id_type=MESH,
+                device_id=wide_peer(to), device_id_type=MESH,
             ).start()
 
     def all_wide(src, dst, sem_s, sem_r):

time: 203 us -> 201 us (level)
  no operation moved by 1% of the time
where the time goes in v5:
time: 201 us
  Pallas kernels  195 us (97%)
  local copies, waits for them, and re-layouts  5.57 us (3%)
    pallas_call x1, Pallas kernels, per_device(): pl.pallas_call(centroid_kernel, out_shape=(jax.ShapeDtypeStruct((clusters...  195 us
    unnamed x7, local copies, waits for them, and re-layouts  5.57 us

profile of v5, /device:TPU:1, one launch (start us, length us, event | category | flops | bytes accessed | tf_op | source)
XLA Modules:
  0.0 200.8 jit_solution(3953032132048945855)
XLA Ops:
  0.6 194.5 %shard_map.103 = (f32[256,1536]{1,0:T(8,128)}, f32[128,1536]{1,0:T(8,128)}, f32[256,1536]{1,0:T(8,128)}) custom-call(bf16[2048,1536]{1,0:T(8,128)(2,1)} %emb_hbm.1, s32[1,2048]{1,0:T(1,128)} %bitcast.5, s32[1,2048]{1,0:T(1,128)} %bitcast.6, s32[1,2048]{1,0:T(1,128)} %bitcast.7, s32[1,256]{1,0:T(1,128)} %bitcast.8, s32[1,128]{1,0:T(1,128)} %bitcast.9, ...), custom_call_target="tpu_custom_call" | custom-call | tf_op jit(solution)/shard_map/pallas_call | solution.py:718
  195.2 0.0 copy-start.1
  195.2 2.7 %copy.14 = f32[256,1536]{1,0:T(8,128)} copy(f32[256,1536]{1,0:T(8,128)} %get-tuple-element.6) | data formatting | bytes 3145728
  197.9 0.0 copy-done.1
  197.9 0.0 copy-start
  197.9 0.9 copy.15
  198.8 0.8 copy-done
  199.6 1.1 copy.16
Async XLA Ops:
  195.2 2.7 %copy-start.1 = (f32[128,1536]{1,0:T(8,128)S(1)}, f32[128,1536]{1,0:T(8,128)}, u32[]{:S(2)}) copy-start(f32[128,1536]{1,0:T(8,128)} %get-tuple-element.7) | copy-start | bytes 2359300
  197.9 1.7 copy-start
